TPU v7x, 32 devices: a whole 2x2x4 slice. The times are simulated.
32 devices in a mesh: dp: 8 (over y, x, core), shard: 4 (over z).
Axes of the slice: x: 2, y: 2, z: 4, core: 2. Of those that a mesh axis runs over, the one named last changes fastest.
Arguments:
- queries: bfloat16 [4096, 2048], P(('dp', 'shard')), may hold values from -6 to 6
- keys_in: bfloat16 [4096, 2048], P(('dp', 'shard')), may hold values from -6 to 6
- values: bfloat16 [4096, 2048], P(('dp', 'shard')), may hold values from -6 to 6
- out_grad: bfloat16 [4096, 2048], P(('dp', 'shard')), may hold values from -48 to 48
- out_weight: bfloat16 [2048, 2048], P('shard'), may hold values from -0.125 to 0.125
- block_lists: int32 [8, 4, 4], P('dp'), may hold values from 0 to 3, as said below
- voxel_count: int32 [8], P('dp'), may hold values from 256 to 512
Outputs:
- grad_query: bfloat16 [4096, 2048], P(('dp', 'shard'))
- grad_key: bfloat16 [4096, 2048], P(('dp', 'shard'))
- grad_value: bfloat16 [4096, 2048], P(('dp', 'shard'))
- grad_weight: bfloat16 [2048, 2048], P('shard')
Inputs may be any that keep to these rules, and one draw needn't show every extreme that they name: `block_lists`: entry 0 of row b of a scene's list is b itself; the 4 entries of a row are different blocks of that scene.
All inputs are finite; a program needn't handle non-finite values.
Results may differ from a plain program's by a relative error of at most 0.0095.
Values may be sent and summed in bfloat16 or wider, within the bound.
No kernel may reach another device: no remote copies, remote signals or barrier semaphores. Data moves between devices by JAX's collectives and lax.ppermute only.
A program may use at most 128 MiB of HBM per device.

v0:
```python
import functools
import math

import jax
import jax.numpy as jnp
from jax import lax
from jax.experimental import pallas as pl
from jax.experimental.pallas import tpu as pltpu
from jax.sharding import PartitionSpec as P

HDIM = 128
BLOCK = 128
NB = 4
MIB = 1024 * 1024
DP = ("chips", "core")

Z, COUNT, CORE, CHIP = range(4)

EARLY = 3

NO_COST = pl.CostEstimate(flops=0, bytes_accessed=1024, transcendentals=0)

f32 = jnp.float32
bf16 = jnp.bfloat16


def dot(a, b, ca, cb):
    return lax.dot_general(a, b, (((ca,), (cb,)), ((), ())), preferred_element_type=f32)


def sds(shape, dtype):
    return jax.ShapeDtypeStruct(shape, dtype)


def params(mib=8):
    return pltpu.CompilerParams(vmem_limit_bytes=mib * MIB)


def swap(x, axis, size, flip):
    return lax.ppermute(x, axis, [(i, i ^ flip) for i in range(size)])


def after(x, *earlier):
    return lax.optimization_barrier((x, *earlier))[0]


def run_all(copies):
    for copy in copies:
        copy.start()
    for copy in copies:
        copy.wait()


def whole(kernel, out_shape, operands, name, scalars=0, mib=8, scratch=()):
    return pl.pallas_call(
        kernel,
        out_shape=out_shape,
        in_specs=[pl.BlockSpec(memory_space=pltpu.SMEM)] * scalars
        + [pl.BlockSpec(memory_space=pltpu.VMEM)] * (len(operands) - scalars),
        out_specs=jax.tree.map(lambda _: pl.BlockSpec(memory_space=pltpu.VMEM), out_shape),
        scratch_shapes=scratch,
        compiler_params=params(mib),
        cost_estimate=NO_COST,
        name=name,
    )(*operands)


def pack_kernel(meta, q_ref, k_ref, v_ref, *refs):
    *outs, sems = refs
    width = outs[0].shape[2]
    copies = []
    for n, out_ref in enumerate(outs):
        k, first = (n, 0) if n < 2 else (n // 2 + 1, n % 2 * EARLY * HDIM)
        start = pl.multiple_of((meta[Z] ^ k) * width + first, 128)
        for i, ref in enumerate((q_ref, k_ref, v_ref)):
            part = ref.at[:, pl.ds(start, out_ref.shape[2])]
            copies.append(pltpu.make_async_copy(part, out_ref.at[i], sems.at[3 * n + i]))
    run_all(copies)


def pack(meta, queries, keys_in, values):
    rows, width = queries.shape
    part, early = width // 4, EARLY * HDIM
    shapes = [sds((3, rows, n), bf16) for n in (part, part, early, part - early, early, part - early)]
    return pl.pallas_call(
        pack_kernel,
        out_shape=shapes,
        in_specs=[pl.BlockSpec(memory_space=pltpu.SMEM)] + [pl.BlockSpec(memory_space=pl.ANY)] * 3,
        out_specs=[pl.BlockSpec(memory_space=pltpu.VMEM)] * len(shapes),
        scratch_shapes=[pltpu.SemaphoreType.DMA((3 * len(shapes),))],
        compiler_params=params(),
        cost_estimate=NO_COST,
        name="pack_heads",
    )(meta, queries, keys_in, values)


def token_pos(shape, dim, z, start=0):
    return (lax.broadcasted_iota(jnp.int32, shape, dim) + start) ^ (z * BLOCK)


def grad_attn_kernel(start, meta, *refs):
    *grads, w_ref, out_ref = refs
    grad = jnp.concatenate([g[...] for g in grads], axis=0)
    live = token_pos((grad.shape[0], 1), 0, meta[Z], start) < meta[COUNT]
    tile = 2 * HDIM

    @pl.loop(0, w_ref.shape[0] // tile)
    def _(i):
        part = pl.ds(pl.multiple_of(i * tile, tile), tile)
        out_ref[:, part] = jnp.where(live, dot(grad, w_ref[part, :], 1, 1), 0.0).astype(bf16)


def grad_attn(meta, grads, weight, start):
    shape = (sum(g.shape[0] for g in grads), weight.shape[0])
    kernel = functools.partial(grad_attn_kernel, start)
    return whole(kernel, sds(shape, bf16), (meta, *grads, weight), "grad_attn", 1, 16)


def head_of(pieces, group, h):
    part = pieces[-1].shape[2]
    parts = []
    for p in pieces:
        start = (group * EARLY * HDIM if p.shape[2] > part else 0) + h * HDIM
        parts.append([p[i, :, start : start + HDIM] for i in range(3)])
    return (jnp.concatenate(x, axis=0) for x in zip(*parts))


def forward_kernel(group, meta, p0, p1, p2, p3, weight_ref, inverse_ref, out_ref, heads_ref, bias_ref):
    pieces = (p0, p1, p2, p3)
    rows = p0.shape[1]
    total = 4 * rows
    tile = 2 * rows
    to_power = math.log2(math.e) / math.sqrt(HDIM)
    query_live = token_pos((1, total), 1, meta[Z]) < meta[COUNT]
    key_live = token_pos((total, 1), 0, meta[Z]) < meta[COUNT]
    bias_ref[...] = jnp.where(key_live | ~query_live, 0.0, -jnp.inf)
    for h in range(p3.shape[2] // HDIM):
        cols = slice(h * HDIM, (h + 1) * HDIM)
        query, key, value = head_of(pieces, group, h)
        for t in range(2):
            part = slice(t * tile, (t + 1) * tile)
            scores = dot(key, query[part], 1, 1) + bias_ref[:, part]
            peak = jnp.max(scores, axis=0, keepdims=True)
            weights = jnp.exp2((scores - peak) * to_power).astype(bf16)
            weight_ref[h, :, part] = weights
            inverse = 1.0 / jnp.sum(weights.astype(f32), axis=0, keepdims=True)
            inverse_ref[h, :, part] = inverse
            heads = dot(value, weights, 0, 0) * inverse
            out_ref[cols, part] = heads
            heads_ref[cols, part] = jnp.where(query_live[:, part], heads, 0.0).astype(bf16)


def forward(meta, pieces, group):
    _, rows, width = pieces[-1].shape
    total = 4 * rows
    shapes = [
        sds((width // HDIM, total, total), bf16),
        sds((width // HDIM, 1, total), f32),
        sds((width, total), f32),
        sds((width, total), bf16),
    ]
    scratch = [pltpu.VMEM((total, total), f32)]
    kernel = functools.partial(forward_kernel, group)
    return whole(kernel, shapes, (meta, *pieces), "attend_forward", 1, 16, scratch)


def gradients(group, pieces, grad_refs, saved, backs):
    weight_ref, inverse_ref, out_ref = saved
    rows = pieces[0].shape[1]
    total = 4 * rows
    tile = 2 * rows
    scale = 1.0 / math.sqrt(HDIM)
    for h in range(pieces[-1].shape[2] // HDIM):
        query, key, value = head_of(pieces, group, h)
        cols = slice(h * HDIM, (h + 1) * HDIM)
        start = (group * EARLY + h) * HDIM
        grad = jnp.concatenate([ref[:, start : start + HDIM] for ref in grad_refs], axis=0)
        grad_key = grad_value = jnp.zeros((total, HDIM), f32)
        for t in range(2):
            span = slice(t * tile, (t + 1) * tile)
            weights = weight_ref[h, :, span]
            inverse = inverse_ref[h, :, span]
            turned = grad[span].astype(f32).T
            row_delta = jnp.sum(out_ref[cols, span] * turned, axis=0, keepdims=True)
            grad_prob = dot(value, grad[span], 1, 1)
            dscore = (weights.astype(f32) * ((grad_prob - row_delta) * (inverse * scale))).astype(bf16)
            grad_query = dot(key, dscore, 0, 0).T.astype(bf16)
            backs[2 * t][0, :, cols] = grad_query[:rows]
            backs[2 * t + 1][0, :, cols] = grad_query[rows:]
            grad_key += dot(dscore, query[span], 1, 0)
            grad_value += dot(weights, (turned * inverse).T.astype(bf16), 1, 0)
        for k in range(4):
            mine = slice(k * rows, (k + 1) * rows)
            backs[k][1, :, cols] = grad_key[mine].astype(bf16)
            backs[k][2, :, cols] = grad_value[mine].astype(bf16)


def backward_early_kernel(*refs):
    gradients(0, refs[:4], refs[4:6], refs[6:9], refs[9:])


def backward_early(pieces, grads, saved):
    shapes = [sds(pieces[-1].shape, bf16)] * 4
    return whole(backward_early_kernel, shapes, (*pieces, *grads, *saved), "backward_early", 0, 16)


def backward_late_kernel(meta, *refs):
    others, back_ref, own = refs[9:13], refs[13], refs[14:]
    gradients(1, refs[:4], refs[4:6], refs[6:9], own)
    first = others[0].shape[2]
    for k in range(4):
        place = meta[Z] ^ k
        back_ref[place, :, :, :first] = others[k][...]
        back_ref[place, :, :, first:] = own[k][...]


def backward_late(meta, pieces, grads, saved, others):
    _, rows, part = pieces[-1].shape
    shape = sds((4, 3, rows, others[0].shape[2] + part), bf16)
    operands = (meta, *pieces, *grads, *saved, *others)
    scratch = [pltpu.VMEM((3, rows, part), bf16)] * 4
    return whole(backward_late_kernel, shape, operands, "backward_late", 1, 16, scratch)


LINE = HDIM // 8


def line_at(meta, head, other, j):
    at = head * HDIM + ((meta[CORE] ^ other) * 4 + (meta[CHIP] ^ j)) * LINE
    return pl.ds(pl.multiple_of(at, LINE), LINE)


def weight_kernel(meta, heads_a, heads_b, *refs):
    *grads, send_ref, keep_ref = refs
    width = heads_a.shape[0] + heads_b.shape[0]
    lines = []
    for other in (1, 0):
        for j in range(4):
            for ref in (heads_a, heads_b):
                lines += [ref[line_at(meta, h, other, j), :] for h in range(ref.shape[0] // HDIM)]
    lines = jnp.concatenate(lines, axis=0)
    tile = 4 * HDIM

    @pl.loop(0, send_ref.shape[1] // tile)
    def _(i):
        part = pl.ds(pl.multiple_of(i * tile, tile), tile)
        product = dot(lines, jnp.concatenate([g[:, part] for g in grads], axis=0), 1, 0)
        send_ref[:, part] = product[: width // 2].astype(bf16)
        keep_ref[:, part] = product[width // 2 :]


def weight_halves(meta, heads, grads):
    shape = (sum(x.shape[0] for x in heads) // 2, grads[0].shape[1])
    return whole(weight_kernel, [sds(shape, bf16), sds(shape, f32)], (meta, *heads, *grads), "weight_halves", 1, 16)


def add_kernel(keep_ref, recv_ref, *outs):
    size = outs[0].shape[0]
    for j, out_ref in enumerate(outs):
        part = slice(j * size, (j + 1) * size)
        out_ref[...] = (keep_ref[part, :] + recv_ref[part, :].astype(f32)).astype(out_ref.dtype)


def add_parts(keep, recv):
    shape = (keep.shape[0] // 4, keep.shape[1])
    return whole(add_kernel, [sds(shape, f32)] + [sds(shape, bf16)] * 3, (keep, recv), "add_parts")


def total_kernel(scale, own_ref, r1, r2, r3, out_ref):
    total = own_ref[...] + r1[...].astype(f32) + r2[...].astype(f32) + r3[...].astype(f32)
    out_ref[...] = (total * scale).astype(bf16)


def total_of(own, recvs, scale):
    return whole(functools.partial(total_kernel, scale), sds(own.shape, bf16), (own, *recvs), "scene_mean")


def join_weight_kernel(meta, *refs):
    *parts, out_ref, sems = refs
    copies = []
    for n, ref in enumerate(parts):
        for h in range(ref.shape[0] // LINE):
            line = out_ref.at[line_at(meta, h, n // 4, n % 4), :]
            part = ref.at[pl.ds(h * LINE, LINE), :]
            copies.append(pltpu.make_async_copy(part, line, sems.at[len(copies)]))
    run_all(copies)


def join_weight(meta, parts):
    size, outw = parts[0].shape
    return pl.pallas_call(
        join_weight_kernel,
        out_shape=sds((8 * size, outw), bf16),
        in_specs=[pl.BlockSpec(memory_space=pltpu.SMEM)] + [pl.BlockSpec(memory_space=pltpu.VMEM)] * 8,
        out_specs=pl.BlockSpec(memory_space=pl.ANY),
        scratch_shapes=[pltpu.SemaphoreType.DMA((8 * size // LINE,))],
        compiler_params=params(),
        cost_estimate=NO_COST,
        name="join_weight",
    )(meta, *parts)


def join_kernel(back_ref, *refs):
    *outs, sems = refs
    width = back_ref.shape[3]
    copies = []
    for j in range(4):
        for i, out_ref in enumerate(outs):
            cols = out_ref.at[:, pl.ds(j * width, width)]
            copies.append(pltpu.make_async_copy(back_ref.at[j, i], cols, sems.at[len(copies)]))
    run_all(copies)


def join(back):
    _, _, rows, width = back.shape
    return pl.pallas_call(
        join_kernel,
        out_shape=[sds((rows, 4 * width), bf16)] * 3,
        in_specs=[pl.BlockSpec(memory_space=pltpu.VMEM)],
        out_specs=[pl.BlockSpec(memory_space=pl.ANY)] * 3,
        scratch_shapes=[pltpu.SemaphoreType.DMA((12,))],
        compiler_params=params(),
        cost_estimate=NO_COST,
        name="join_heads",
    )(back)


def dense_body(queries, keys_in, values, out_grad, out_weight, voxel_count):
    meta = jnp.stack([lax.axis_index("shard"), voxel_count[0], lax.axis_index("core"), lax.axis_index("chips")])
    meta = meta.astype(jnp.int32)

    def send(x, k, *earlier):
        return swap(after(x, *earlier) if earlier else x, "shard", 4, k)

    across = send(out_grad, 2)
    beside = send(out_grad, 1)
    own, near1, far2a, far2b, far3a, far3b = pack(meta, queries, keys_in, values)
    piece1 = send(near1, 1)
    piece3a = send(far3a, 3, beside)
    piece2a = send(far2a, 2, across)
    piece3b = send(far3b, 3, piece3a)
    piece2b = send(far2b, 2, piece2a)
    half = across.shape[0] // 2
    corners = [send(across[:half], 1), send(after(across, piece1)[half:], 1)]
    grad_early = grad_attn(meta, (out_grad, beside, across), out_weight, 0)

    pieces = (own, piece1, piece2a, piece3a)
    *saved, heads_a = forward(meta, pieces, 0)
    grad_early, heads_a, *corners = lax.optimization_barrier((grad_early, heads_a, *corners))
    grads = (out_grad, beside, across, *corners)
    grad_heads = (grad_early, grad_attn(meta, grads[3:], out_weight, 3 * BLOCK))
    mine = backward_early(pieces, grad_heads, saved)
    *mine, piece2b, piece3b = lax.optimization_barrier((*mine, piece2b, piece3b))
    pieces = (own, piece1, piece2b, piece3b)
    *saved, heads_b = forward(meta, pieces, 1)
    back = backward_late(meta, pieces, grad_heads, saved, mine)
    back_all = lax.all_to_all(back, "shard", split_axis=0, concat_axis=0, tiled=True)

    out, keep = weight_halves(meta, (heads_a, after(heads_b, back)), grads)
    own_part, *sends = add_parts(keep, swap(out, "core", 2, 1))
    recvs = [swap(x, "chips", 4, j + 1) for j, x in enumerate(sends)]
    done = total_of(own_part, recvs, 1.0 / 8)
    near = [done] + [swap(done, "chips", 4, j) for j in (1, 2, 3)]
    far = [swap(x, "core", 2, 1) for x in near]
    grad_weight = join_weight(meta, near + far)
    return (*join(back_all), grad_weight)


def attend_listed(queries, keys_in, values, block_ids, live_count):
    row_count, width_all = queries.shape
    head_count = width_all // HDIM
    block_count = row_count // BLOCK
    score_scale = 1.0 / math.sqrt(HDIM)
    query_blk = queries.reshape(block_count, BLOCK, head_count, HDIM)
    key_blk = keys_in.reshape(block_count, BLOCK, head_count, HDIM)[block_ids].reshape(
        block_count, NB * BLOCK, head_count, HDIM
    )
    value_blk = values.reshape(block_count, BLOCK, head_count, HDIM)[block_ids].reshape(
        block_count, NB * BLOCK, head_count, HDIM
    )
    query_pos = jnp.arange(row_count, dtype=jnp.int32).reshape(block_count, BLOCK)
    key_pos = (
        block_ids[:, :, None] * BLOCK + jnp.arange(BLOCK, dtype=jnp.int32)[None, None, :]
    ).reshape(block_count, NB * BLOCK)
    allowed = (key_pos[:, None, :] < live_count) | (query_pos[:, :, None] >= live_count)
    scores = (
        jnp.einsum("bqhd,bkhd->bhqk", query_blk, key_blk, preferred_element_type=jnp.float32)
        * score_scale
    )
    scores = jnp.where(allowed[:, None], scores, -jnp.inf)
    peak = jnp.max(scores, axis=-1, keepdims=True)
    weights = jnp.exp(scores - peak)
    probs = weights / jnp.sum(weights, axis=-1, keepdims=True)
    return (query_blk, key_blk, value_blk, probs)


def listed_body(queries, keys_in, values, out_grad, out_weight, block_lists, voxel_count):
    local_rows = queries.shape[0]
    live_count = voxel_count[0]
    block_ids = block_lists[0]
    positions = lax.axis_index("shard") * local_rows + jnp.arange(local_rows, dtype=jnp.int32)
    grad_live = jnp.where((positions < live_count)[:, None], out_grad, jnp.zeros_like(out_grad))
    query_head, key_head, value_head = (
        lax.all_to_all(queries, "shard", split_axis=1, concat_axis=0, tiled=True),
        lax.all_to_all(keys_in, "shard", split_axis=1, concat_axis=0, tiled=True),
        lax.all_to_all(values, "shard", split_axis=1, concat_axis=0, tiled=True),
    )
    row_count, width_all = query_head.shape
    head_count = width_all // HDIM
    block_count = row_count // BLOCK
    score_scale = 1.0 / math.sqrt(HDIM)
    query_blk, key_blk, value_blk, probs = attend_listed(
        query_head, key_head, value_head, block_ids, live_count
    )
    prob_bf = probs.astype(jnp.bfloat16)
    heads_out = (
        jnp.einsum("bhqk,bkhd->bqhd", prob_bf, value_blk, preferred_element_type=jnp.float32)
        .reshape(row_count, width_all)
        .astype(jnp.bfloat16)
    )
    row_piece = lax.all_gather(grad_live, "shard", axis=0, tiled=True)
    acc_now = jnp.einsum("rw,ro->wo", heads_out, row_piece, preferred_element_type=jnp.float32)
    product = jnp.einsum("ro,wo->rw", row_piece, out_weight, preferred_element_type=jnp.float32)
    grad_o = product.astype(jnp.bfloat16).reshape(block_count, BLOCK, head_count, HDIM)
    grad_prob = jnp.einsum("bqhd,bkhd->bhqk", grad_o, value_blk, preferred_element_type=jnp.float32)
    row_delta = jnp.sum(probs * grad_prob, axis=-1, keepdims=True)
    dscore = (probs * (grad_prob - row_delta) * score_scale).astype(jnp.bfloat16)
    grad_query = (
        jnp.einsum("bhqk,bkhd->bqhd", dscore, key_blk, preferred_element_type=jnp.float32)
        .reshape(row_count, width_all)
        .astype(jnp.bfloat16)
    )
    onehot = (
        block_ids[:, :, None] == jnp.arange(block_count, dtype=jnp.int32)[None, None, :]
    ).astype(jnp.float32)
    key_parts = jnp.einsum(
        "bhqk,bqhd->bkhd", dscore, query_blk, preferred_element_type=jnp.float32
    ).reshape(block_count, NB, BLOCK, width_all)
    value_parts = jnp.einsum(
        "bhqk,bqhd->bkhd", prob_bf, grad_o, preferred_element_type=jnp.float32
    ).reshape(block_count, NB, BLOCK, width_all)
    grad_key = (
        jnp.einsum("bjc,bjrx->crx", onehot, key_parts, precision=lax.Precision.HIGHEST)
        .reshape(row_count, width_all)
        .astype(jnp.bfloat16)
    )
    grad_value = (
        jnp.einsum("bjc,bjrx->crx", onehot, value_parts, precision=lax.Precision.HIGHEST)
        .reshape(row_count, width_all)
        .astype(jnp.bfloat16)
    )
    query_back, key_back, value_back = (
        lax.all_to_all(grad_query, "shard", split_axis=0, concat_axis=1, tiled=True),
        lax.all_to_all(grad_key, "shard", split_axis=0, concat_axis=1, tiled=True),
        lax.all_to_all(grad_value, "shard", split_axis=0, concat_axis=1, tiled=True),
    )
    scene_total = lax.axis_size(DP)
    summed = lax.psum(acc_now, DP)
    grad_weight = (summed / scene_total).astype(jnp.bfloat16)
    return (query_back, key_back, value_back, grad_weight)


def body(queries, keys_in, values, out_grad, out_weight, block_lists, voxel_count):
    dense = block_lists.shape[1] == NB and queries.shape[0] == BLOCK
    if dense and lax.axis_size("shard") == 4 and lax.axis_size("chips") == 4:
        return dense_body(queries, keys_in, values, out_grad, out_weight, voxel_count)
    return listed_body(queries, keys_in, values, out_grad, out_weight, block_lists, voxel_count)


def solution(mesh):
    chips = mesh.shape["dp"] // 2
    mesh = jax.sharding.Mesh(mesh.devices.reshape(chips, 2, -1), ("chips", "core", "shard"))
    return jax.shard_map(
        body,
        mesh=mesh,
        in_specs=(
            P((*DP, "shard"), None),
            P((*DP, "shard"), None),
            P((*DP, "shard"), None),
            P((*DP, "shard"), None),
            P("shard", None),
            P(DP, None, None),
            P(DP),
        ),
        out_specs=(
            P((*DP, "shard"), None),
            P((*DP, "shard"), None),
            P((*DP, "shard"), None),
            P("shard", None),
        ),
        check_vma=False,
    )
```

profile of v0, /device:TPU:0, one launch (start us, length us, event | category | flops | bytes accessed | tf_op | source)
XLA Modules:
  0.0 118.6 jit_solution(1617781226263751103)
XLA Ops:
  0.6 0.0 copy-start.1
  0.6 0.0 copy-start
  0.7 3.1 %collective-permute-start.3 = (bf16[128,2048]{1,0:T(8,128)(2,1)}, bf16[128,2048]{1,0:T(8,128)(2,1)}, u32[]{:S(2)}, u32[]{:S(2)}) collective-permute-start(bf16[128,2048]{1,0:T(8,128)(2,1)} %refs_0_.3), channel_id=1, source_target_pairs={{0,1},{1,0},{2,3},{3,2},{4,5},{5,4},{6,7},{7,6},{8,9},{9,8},{10,11... | collective-permute-start | bytes 1572872 | tf_op jit(solution)/shard_map/ppermute | solution.py:40
  3.7 2.6 %collective-permute-start.1 = (bf16[128,2048]{1,0:T(8,128)(2,1)}, bf16[128,2048]{1,0:T(8,128)(2,1)S(1)}, u32[]{:S(2)}, u32[]{:S(2)}) collective-permute-start(bf16[128,2048]{1,0:T(8,128)(2,1)} %refs_0_.3), channel_id=1, source_target_pairs={{0,2},{1,3},{2,0},{3,1},{4,6},{5,7},{6,4},{7,5},{8,10},{9,11},{10,... | collective-permute-start | bytes 1572872 | tf_op jit(solution)/shard_map/ppermute | solution.py:40
  7.0 0.1 pad_add_fusion.meta
  7.1 1.0 copy-done.4
  8.1 1.0 copy-done.5
  9.1 1.0 copy-done.6
  10.2 1.0 pack_heads.1
  11.2 0.5 collective-permute-start
  11.7 16.2 %collective-permute-done.3.refs_1_ = bf16[128,2048]{1,0:T(8,128)(2,1)} collective-permute-done((bf16[128,2048]{1,0:T(8,128)(2,1)}, bf16[128,2048]{1,0:T(8,128)(2,1)}, u32[]{:S(2)}, u32[]{:S(2)}) %collective-permute-start.3) | collective-permute-done | bytes 524320 | tf_op jit(solution)/shard_map/ppermute | solution.py:40
  27.9 3.6 %collective-permute-start.4 = (bf16[3,128,384]{2,1,0:T(8,128)(2,1)S(1)}, bf16[3,128,384]{2,1,0:T(8,128)(2,1)S(1)}, u32[]{:S(2)}, u32[]{:S(2)}) collective-permute-start(bf16[3,128,384]{2,1,0:T(8,128)(2,1)S(1)} %get-tuple-element.52), channel_id=1, source_target_pairs={{0,3},{1,2},{2,1},{3,0},{4,7},{5,6},{6,5},{7,4},{8,11},{9,10},{10,... | collective-permute-start | bytes 884744 | tf_op jit(solution)/shard_map/ppermute | solution.py:40
  31.5 0.0 collective-permute-done.1.refs_2_
  31.5 0.0 collective-permute-start.2
  31.5 2.0 %collective-permute-start.5 = (bf16[64,2048]{1,0:T(8,128)(2,1)S(1)}, bf16[64,2048]{1,0:T(8,128)(2,1)S(1)}, u32[]{:S(2)}, u32[]{:S(2)}) collective-permute-start(bf16[64,2048]{1,0:T(8,128)(2,1)S(1)} %slice.8), channel_id=1, source_target_pairs={{0,1},{1,0},{2,3},{3,2},{4,5},{5,4},{6,7},{7,6},{8,9},{9,8},{10,11... | collective-permute-start | bytes 786440 | tf_op jit(solution)/shard_map/ppermute | solution.py:40
  33.5 10.6 %collective-permute-done.p1.refs_1_ = bf16[3,128,512]{2,1,0:T(8,128)(2,1)S(1)} collective-permute-done((bf16[3,128,512]{2,1,0:T(8,128)(2,1)S(1)}, bf16[3,128,512]{2,1,0:T(8,128)(2,1)S(1)}, u32[]{:S(2)}, u32[]{:S(2)}) %collective-permute-start) | collective-permute-done | bytes 393248 | tf_op jit(solution)/shard_map/ppermute | solution.py:40
  44.1 0.1 collective-permute-start.6
  44.2 1.2 collective-permute-done.4.p3.refs_3_
  45.3 3.0 %collective-permute-start.8 = (bf16[3,128,128]{2,1,0:T(8,128)(2,1)S(1)}, bf16[3,128,128]{2,1,0:T(8,128)(2,1)S(1)}, u32[]{:S(2)}, u32[]{:S(2)}) collective-permute-start(bf16[3,128,128]{2,1,0:T(8,128)(2,1)S(1)} %get-tuple-element.68), channel_id=1, source_target_pairs={{0,3},{1,2},{2,1},{3,0},{4,7},{5,6},{6,5},{7,4},{8,11},{9,10},{10,... | collective-permute-start | bytes 294920 | tf_op jit(solution)/shard_map/ppermute | solution.py:40
  48.3 7.6 %collective-permute-done.2.p2.refs_2_ = bf16[3,128,384]{2,1,0:T(8,128)(2,1)S(1)} collective-permute-done((bf16[3,128,384]{2,1,0:T(8,128)(2,1)S(1)}, bf16[3,128,384]{2,1,0:T(8,128)(2,1)S(1)}, u32[]{:S(2)}, u32[]{:S(2)}) %collective-permute-start.2) | collective-permute-done | bytes 294944 | tf_op jit(solution)/shard_map/ppermute | solution.py:40
  55.9 0.0 collective-permute-start.7
  55.9 0.0 copy-done.1
  56.0 2.4 %grad_attn.2.refs_4_ = bf16[384,512]{1,0:T(8,128)(2,1)S(1)} custom-call(s32[4]{0:T(128)S(1)} %pad_add_fusion.meta, bf16[128,2048]{1,0:T(8,128)(2,1)S(1)} %copy-done.1, bf16[128,2048]{1,0:T(8,128)(2,1)} %collective-permute-done.3.refs_1_, bf16[128,2048]{1,0:T(8,128)(2,1)S(1)} %collective-permute-done.1.refs_2_, bf16[512,2048]{1,0:T(8,128)(2,1)S(1)} %copy-done), custom_call_target="tpu_custom_call" | custom-call | bytes 1024 | tf_op jit(solution)/shard_map/grad_attn/pallas_call | solution.py:55
  58.3 3.4 %attend_forward.2 = (bf16[3,512,512]{2,1,0:T(8,128)(2,1)S(1)}, f32[3,1,512]{2,1,0:T(1,128)S(1)}, f32[384,512]{1,0:T(8,128)S(1)}, bf16[384,512]{1,0:T(8,128)(2,1)S(1)}) custom-call(s32[4]{0:T(128)S(1)} %pad_add_fusion.meta, bf16[3,128,512]{2,1,0:T(8,128)(2,1)S(1)} %get-tuple-element.47.p0.refs_0_, bf16[3,128,512]{2,1,0:T(8,128)(2,1)S(1)} %collective-permute-done.p1.refs_1_, ...), custom_call_target="tpu_custom_call" | custom-call | bytes 1024 | tf_op jit(solution)/shard_map/attend_forward/pallas_call | solution.py:55
  61.7 0.0 copy-start.7
  61.7 0.0 collective-permute-done.5.refs_0_.refs_3_
  61.8 0.0 collective-permute-done.6.refs_1_.refs_4_
  61.8 0.0 copy-start.2
  61.8 1.5 %grad_attn.3.refs_5_ = bf16[128,512]{1,0:T(8,128)(2,1)S(1)} custom-call(s32[4]{0:T(128)S(1)} %pad_add_fusion.meta, bf16[64,2048]{1,0:T(8,128)(2,1)S(1)} %collective-permute-done.5.refs_0_.refs_3_, bf16[64,2048]{1,0:T(8,128)(2,1)S(1)} %collective-permute-done.6.refs_1_.refs_4_, bf16[512,2048]{1,0:T(8,128)(2,1)S(1)} %copy-done), custom_call_target="tpu_custom_call" | custom-call | bytes 1024 | tf_op jit(solution)/shard_map/grad_attn/pallas_call | solution.py:55
  63.3 2.8 %backward_early.1 = (bf16[3,128,384]{2,1,0:T(8,128)(2,1)S(1)}, bf16[3,128,384]{2,1,0:T(8,128)(2,1)S(1)}, bf16[3,128,384]{2,1,0:T(8,128)(2,1)S(1)}, bf16[3,128,384]{2,1,0:T(8,128)(2,1)S(1)}) custom-call(bf16[3,128,512]{2,1,0:T(8,128)(2,1)S(1)} %get-tuple-element.47.p0.refs_0_, bf16[3,128,512]{2,1,0:T(8,128)(2,1)S(1)} %collective-permute-done.p1.refs_1_, ...), custom_call_target="tpu_custom_call" | custom-call | bytes 1024 | tf_op jit(solution)/shard_map/backward_early/pallas_call | solution.py:55
  66.1 0.0 collective-permute-done.8.p3.refs_3_
  66.1 0.0 collective-permute-done.7.p2.refs_2_
  66.1 1.6 %attend_forward.3 = (bf16[1,512,512]{2,1,0:T(8,128)(2,1)S(1)}, f32[1,1,512]{2,1,0:T(1,128)S(1)}, f32[128,512]{1,0:T(8,128)S(1)}, bf16[128,512]{1,0:T(8,128)(2,1)S(1)}) custom-call(s32[4]{0:T(128)S(1)} %pad_add_fusion.meta, bf16[3,128,512]{2,1,0:T(8,128)(2,1)S(1)} %get-tuple-element.47.p0.refs_0_, bf16[3,128,512]{2,1,0:T(8,128)(2,1)S(1)} %collective-permute-done.p1.refs_1_, ...), custom_call_target="tpu_custom_call" | custom-call | bytes 1024 | tf_op jit(solution)/shard_map/attend_forward/pallas_call | solution.py:55
  67.8 2.9 %backward_late.1 = bf16[4,3,128,512]{3,2,1,0:T(8,128)(2,1)} custom-call(s32[4]{0:T(128)S(1)} %pad_add_fusion.meta, bf16[3,128,512]{2,1,0:T(8,128)(2,1)S(1)} %get-tuple-element.47.p0.refs_0_, bf16[3,128,512]{2,1,0:T(8,128)(2,1)S(1)} %collective-permute-done.p1.refs_1_, bf16[3,128,128]{2,1,0:T(8,128)(2,1)S(1)} %collective-permute-done.7.p2.refs_2_, ...), custom_call_target="tpu_custom_call" | custom-call | bytes 1024 | tf_op jit(solution)/shard_map/backward_late/pallas_call | solution.py:55
  70.7 6.6 %all-to-all-start = ((bf16[4,3,128,512]{3,2,1,0:T(8,128)(2,1)}), bf16[4,3,128,512]{3,2,1,0:T(8,128)(2,1)S(1)}, u32[]{:S(2)}, u32[]{:S(2)}) async-start(bf16[4,3,128,512]{3,2,1,0:T(8,128)(2,1)} %backward_late.1), calls=%async_computation | async-start | bytes 3145728 | tf_op jit(solution)/shard_map/all_to_all | solution.py:357
  77.2 1.0 copy-done.8
  78.2 2.9 %weight_halves.1 = (bf16[256,2048]{1,0:T(8,128)(2,1)S(1)}, f32[256,2048]{1,0:T(8,128)S(1)}) custom-call(s32[4]{0:T(128)S(1)} %pad_add_fusion.meta, bf16[384,512]{1,0:T(8,128)(2,1)S(1)} %copy-done.8, bf16[128,512]{1,0:T(8,128)(2,1)S(1)} %get-tuple-element.83.heads_b, bf16[128,2048]{1,0:T(8,128)(2,1)S(1)} %copy-done.1, ...), custom_call_target="tpu_custom_call" | custom-call | bytes 1024 | tf_op jit(solution)/shard_map/weight_halves/pallas_call | solution.py:55
  81.1 0.1 collective-permute-start.9
  81.2 2.6 %collective-permute-done.9.recv_ref = bf16[256,2048]{1,0:T(8,128)(2,1)S(1)} collective-permute-done((bf16[256,2048]{1,0:T(8,128)(2,1)S(1)}, bf16[256,2048]{1,0:T(8,128)(2,1)S(1)}, u32[]{:S(2)}, u32[]{:S(2)}) %collective-permute-start.9) | collective-permute-done | bytes 1048608 | tf_op jit(solution)/shard_map/ppermute | solution.py:40
  83.8 0.2 add_parts.1
  84.0 1.6 %collective-permute-start.10 = (bf16[64,2048]{1,0:T(8,128)(2,1)S(1)}, bf16[64,2048]{1,0:T(8,128)(2,1)S(1)}, u32[]{:S(2)}, u32[]{:S(2)}) collective-permute-start(bf16[64,2048]{1,0:T(8,128)(2,1)S(1)} %get-tuple-element.87), channel_id=1, source_target_pairs={{0,8},{8,0},{16,24},{24,16},{1,9},{9,1},{17,25},{25,17},{2,10},{10... | collective-permute-start | bytes 786440 | tf_op jit(solution)/shard_map/ppermute | solution.py:40
  85.6 1.5 %collective-permute-start.11 = (bf16[64,2048]{1,0:T(8,128)(2,1)S(1)}, bf16[64,2048]{1,0:T(8,128)(2,1)S(1)}, u32[]{:S(2)}, u32[]{:S(2)}) collective-permute-start(bf16[64,2048]{1,0:T(8,128)(2,1)S(1)} %get-tuple-element.88), channel_id=1, source_target_pairs={{0,16},{8,24},{16,0},{24,8},{1,17},{9,25},{17,1},{25,9},{2,18},{10... | collective-permute-start | bytes 786440 | tf_op jit(solution)/shard_map/ppermute | solution.py:40
  87.1 0.5 collective-permute-start.12
  87.6 5.7 %collective-permute-done.10.r1 = bf16[64,2048]{1,0:T(8,128)(2,1)S(1)} collective-permute-done((bf16[64,2048]{1,0:T(8,128)(2,1)S(1)}, bf16[64,2048]{1,0:T(8,128)(2,1)S(1)}, u32[]{:S(2)}, u32[]{:S(2)}) %collective-permute-start.10) | collective-permute-done | bytes 262176 | tf_op jit(solution)/shard_map/ppermute | solution.py:40
  93.3 6.0 %collective-permute-done.11.r2 = bf16[64,2048]{1,0:T(8,128)(2,1)S(1)} collective-permute-done((bf16[64,2048]{1,0:T(8,128)(2,1)S(1)}, bf16[64,2048]{1,0:T(8,128)(2,1)S(1)}, u32[]{:S(2)}, u32[]{:S(2)}) %collective-permute-start.11) | collective-permute-done | bytes 262176 | tf_op jit(solution)/shard_map/ppermute | solution.py:40
  99.3 0.0 collective-permute-done.12.r3
  99.3 0.1 scene_mean.1.refs_0_
  99.4 1.6 %collective-permute-start.15 = (bf16[64,2048]{1,0:T(8,128)(2,1)S(1)}, bf16[64,2048]{1,0:T(8,128)(2,1)S(1)}, u32[]{:S(2)}, u32[]{:S(2)}) collective-permute-start(bf16[64,2048]{1,0:T(8,128)(2,1)S(1)} %scene_mean.1.refs_0_), channel_id=1, source_target_pairs={{0,24},{8,16},{16,8},{24,0},{1,25},{9,17},{17,9},{25,1},{2,26},{10... | collective-permute-start | bytes 786440 | tf_op jit(solution)/shard_map/ppermute | solution.py:40
  101.0 1.2 %collective-permute-start.14 = (bf16[64,2048]{1,0:T(8,128)(2,1)S(1)}, bf16[64,2048]{1,0:T(8,128)(2,1)S(1)}, u32[]{:S(2)}, u32[]{:S(2)}) collective-permute-start(bf16[64,2048]{1,0:T(8,128)(2,1)S(1)} %scene_mean.1.refs_0_), channel_id=1, source_target_pairs={{0,16},{8,24},{16,0},{24,8},{1,17},{9,25},{17,1},{25,9},{2,18},{10... | collective-permute-start | bytes 786440 | tf_op jit(solution)/shard_map/ppermute | solution.py:40
  102.2 0.8 collective-permute-start.13
  103.0 0.0 collective-permute-start.16
  103.0 6.7 %collective-permute-done.15.refs_3_ = bf16[64,2048]{1,0:T(8,128)(2,1)S(1)} collective-permute-done((bf16[64,2048]{1,0:T(8,128)(2,1)S(1)}, bf16[64,2048]{1,0:T(8,128)(2,1)S(1)}, u32[]{:S(2)}, u32[]{:S(2)}) %collective-permute-start.15) | collective-permute-done | bytes 262176 | tf_op jit(solution)/shard_map/ppermute | solution.py:40
  109.7 0.0 collective-permute-start.19
  109.7 3.6 %collective-permute-done.14.refs_2_ = bf16[64,2048]{1,0:T(8,128)(2,1)S(1)} collective-permute-done((bf16[64,2048]{1,0:T(8,128)(2,1)S(1)}, bf16[64,2048]{1,0:T(8,128)(2,1)S(1)}, u32[]{:S(2)}, u32[]{:S(2)}) %collective-permute-start.14) | collective-permute-done | bytes 262176 | tf_op jit(solution)/shard_map/ppermute | solution.py:40
  113.3 0.0 collective-permute-start.18
  113.3 0.0 collective-permute-done.13.refs_1_
  113.3 0.5 collective-permute-start.17
  113.8 0.0 collective-permute-done.16.refs_4_
  113.8 0.0 collective-permute-done.19.refs_7_
  113.8 1.0 collective-permute-done.18.refs_6_
  114.9 0.4 collective-permute-done.17.refs_5_
  115.2 2.1 %join_weight.1 = bf16[512,2048]{1,0:T(8,128)(2,1)} custom-call(s32[4]{0:T(128)S(1)} %pad_add_fusion.meta, bf16[64,2048]{1,0:T(8,128)(2,1)S(1)} %scene_mean.1.refs_0_, bf16[64,2048]{1,0:T(8,128)(2,1)S(1)} %collective-permute-done.13.refs_1_, bf16[64,2048]{1,0:T(8,128)(2,1)S(1)} %collective-permute-done.14.refs_2_, ...), custom_call_target="tpu_custom_call" | custom-call | bytes 1024 | tf_op jit(solution)/shard_map/join_weight/pallas_call | solution.py:291
  117.3 0.0 all-to-all-done.back_ref
  117.4 1.2 %join_heads.1 = (bf16[128,2048]{1,0:T(8,128)(2,1)}, bf16[128,2048]{1,0:T(8,128)(2,1)}, bf16[128,2048]{1,0:T(8,128)(2,1)}) custom-call(bf16[4,3,128,512]{3,2,1,0:T(8,128)(2,1)S(1)} %all-to-all-done.back_ref), custom_call_target="tpu_custom_call" | custom-call | bytes 1024 | tf_op jit(solution)/shard_map/join_heads/pallas_call | solution.py:316
  (11 shorter events, 0.1 us)
Async XLA Ops:
  0.6 55.3 %copy-start.1 = (bf16[128,2048]{1,0:T(8,128)(2,1)S(1)}, bf16[128,2048]{1,0:T(8,128)(2,1)}, u32[]{:S(2)}) copy-start(bf16[128,2048]{1,0:T(8,128)(2,1)} %refs_0_.3) | copy-start | bytes 1572868
  0.6 55.3 %copy-start = (bf16[512,2048]{1,0:T(8,128)(2,1)S(1)}, bf16[512,2048]{1,0:T(8,128)(2,1)}, u32[]{:S(2)}) copy-start(bf16[512,2048]{1,0:T(8,128)(2,1)} %refs_2_.1) | copy-start | bytes 6291460
  0.7 27.3 %collective-permute-start.3 = (bf16[128,2048]{1,0:T(8,128)(2,1)}, bf16[128,2048]{1,0:T(8,128)(2,1)}, u32[]{:S(2)}, u32[]{:S(2)}) collective-permute-start(bf16[128,2048]{1,0:T(8,128)(2,1)} %refs_0_.3), channel_id=1, source_target_pairs={{0,1},{1,0},{2,3},{3,2},{4,5},{5,4},{6,7},{7,6},{8,9},{9,8},{10,11... | collective-permute-start | bytes 1572872 | tf_op jit(solution)/shard_map/ppermute | solution.py:40
  3.7 27.8 %collective-permute-start.1 = (bf16[128,2048]{1,0:T(8,128)(2,1)}, bf16[128,2048]{1,0:T(8,128)(2,1)S(1)}, u32[]{:S(2)}, u32[]{:S(2)}) collective-permute-start(bf16[128,2048]{1,0:T(8,128)(2,1)} %refs_0_.3), channel_id=1, source_target_pairs={{0,2},{1,3},{2,0},{3,1},{4,6},{5,7},{6,4},{7,5},{8,10},{9,11},{10,... | collective-permute-start | bytes 1572872 | tf_op jit(solution)/shard_map/ppermute | solution.py:40
  7.1 1.0 copy-start.4
  8.1 1.0 copy-start.5
  9.1 1.0 copy-start.6
  11.2 32.9 %collective-permute-start = (bf16[3,128,512]{2,1,0:T(8,128)(2,1)S(1)}, bf16[3,128,512]{2,1,0:T(8,128)(2,1)S(1)}, u32[]{:S(2)}, u32[]{:S(2)}) collective-permute-start(bf16[3,128,512]{2,1,0:T(8,128)(2,1)S(1)} %get-tuple-element.48), channel_id=1, source_target_pairs={{0,1},{1,0},{2,3},{3,2},{4,5},{5,4},{6,7},{7,6},{8,9},{9,8},{10,11... | collective-permute-start | bytes 1179656 | tf_op jit(solution)/shard_map/ppermute | solution.py:40
  27.9 17.4 %collective-permute-start.4 = (bf16[3,128,384]{2,1,0:T(8,128)(2,1)S(1)}, bf16[3,128,384]{2,1,0:T(8,128)(2,1)S(1)}, u32[]{:S(2)}, u32[]{:S(2)}) collective-permute-start(bf16[3,128,384]{2,1,0:T(8,128)(2,1)S(1)} %get-tuple-element.52), channel_id=1, source_target_pairs={{0,3},{1,2},{2,1},{3,0},{4,7},{5,6},{6,5},{7,4},{8,11},{9,10},{10,... | collective-permute-start | bytes 884744 | tf_op jit(solution)/shard_map/ppermute | solution.py:40
  31.5 24.4 %collective-permute-start.2 = (bf16[3,128,384]{2,1,0:T(8,128)(2,1)S(1)}, bf16[3,128,384]{2,1,0:T(8,128)(2,1)S(1)}, u32[]{:S(2)}, u32[]{:S(2)}) collective-permute-start(bf16[3,128,384]{2,1,0:T(8,128)(2,1)S(1)} %get-tuple-element.50), channel_id=1, source_target_pairs={{0,2},{1,3},{2,0},{3,1},{4,6},{5,7},{6,4},{7,5},{8,10},{9,11},{10,... | collective-permute-start | bytes 884744 | tf_op jit(solution)/shard_map/ppermute | solution.py:40
  31.5 30.2 %collective-permute-start.5 = (bf16[64,2048]{1,0:T(8,128)(2,1)S(1)}, bf16[64,2048]{1,0:T(8,128)(2,1)S(1)}, u32[]{:S(2)}, u32[]{:S(2)}) collective-permute-start(bf16[64,2048]{1,0:T(8,128)(2,1)S(1)} %slice.8), channel_id=1, source_target_pairs={{0,1},{1,0},{2,3},{3,2},{4,5},{5,4},{6,7},{7,6},{8,9},{9,8},{10,11... | collective-permute-start | bytes 786440 | tf_op jit(solution)/shard_map/ppermute | solution.py:40
  44.1 17.7 %collective-permute-start.6 = (bf16[64,2048]{1,0:T(8,128)(2,1)S(1)}, bf16[64,2048]{1,0:T(8,128)(2,1)S(1)}, u32[]{:S(2)}, u32[]{:S(2)}) collective-permute-start(bf16[64,2048]{1,0:T(8,128)(2,1)S(1)} %slice.7), channel_id=1, source_target_pairs={{0,1},{1,0},{2,3},{3,2},{4,5},{5,4},{6,7},{7,6},{8,9},{9,8},{10,11... | collective-permute-start | bytes 786440 | tf_op jit(solution)/shard_map/ppermute | solution.py:40
  45.3 20.8 %collective-permute-start.8 = (bf16[3,128,128]{2,1,0:T(8,128)(2,1)S(1)}, bf16[3,128,128]{2,1,0:T(8,128)(2,1)S(1)}, u32[]{:S(2)}, u32[]{:S(2)}) collective-permute-start(bf16[3,128,128]{2,1,0:T(8,128)(2,1)S(1)} %get-tuple-element.68), channel_id=1, source_target_pairs={{0,3},{1,2},{2,1},{3,0},{4,7},{5,6},{6,5},{7,4},{8,11},{9,10},{10,... | collective-permute-start | bytes 294920 | tf_op jit(solution)/shard_map/ppermute | solution.py:40
  55.9 10.2 %collective-permute-start.7 = (bf16[3,128,128]{2,1,0:T(8,128)(2,1)S(1)}, bf16[3,128,128]{2,1,0:T(8,128)(2,1)S(1)}, u32[]{:S(2)}, u32[]{:S(2)}) collective-permute-start(bf16[3,128,128]{2,1,0:T(8,128)(2,1)S(1)} %get-tuple-element.66), channel_id=1, source_target_pairs={{0,2},{1,3},{2,0},{3,1},{4,6},{5,7},{6,4},{7,5},{8,10},{9,11},{10,... | collective-permute-start | bytes 294920 | tf_op jit(solution)/shard_map/ppermute | solution.py:40
  61.7 4.4 %copy-start.7 = (bf16[384,512]{1,0:T(8,128)(2,1)}, bf16[384,512]{1,0:T(8,128)(2,1)S(1)}, u32[]{:S(2)}) copy-start(bf16[384,512]{1,0:T(8,128)(2,1)S(1)} %get-tuple-element.81.heads_a) | copy-start | bytes 1179652
  61.8 4.3 %copy-start.2 = (bf16[64,2048]{1,0:T(8,128)(2,1)}, bf16[64,2048]{1,0:T(8,128)(2,1)S(1)}, u32[]{:S(2)}) copy-start(bf16[64,2048]{1,0:T(8,128)(2,1)S(1)} %collective-permute-done.6.refs_1_.refs_4_) | copy-start | bytes 786436
  70.7 6.6 %copy-start.3 = (bf16[64,2048]{1,0:T(8,128)(2,1)S(1)}, bf16[64,2048]{1,0:T(8,128)(2,1)}, u32[]{:S(2)}) copy-start(bf16[64,2048]{1,0:T(8,128)(2,1)} %copy-done.2) | copy-start | bytes 786436
  70.7 46.7 %all-to-all-start = ((bf16[4,3,128,512]{3,2,1,0:T(8,128)(2,1)}), bf16[4,3,128,512]{3,2,1,0:T(8,128)(2,1)S(1)}, u32[]{:S(2)}, u32[]{:S(2)}) async-start(bf16[4,3,128,512]{3,2,1,0:T(8,128)(2,1)} %backward_late.1), calls=%async_computation | async-start | bytes 3145728 | tf_op jit(solution)/shard_map/all_to_all | solution.py:357
  77.2 1.0 copy-start.8
  81.1 2.7 %collective-permute-start.9 = (bf16[256,2048]{1,0:T(8,128)(2,1)S(1)}, bf16[256,2048]{1,0:T(8,128)(2,1)S(1)}, u32[]{:S(2)}, u32[]{:S(2)}) collective-permute-start(bf16[256,2048]{1,0:T(8,128)(2,1)S(1)} %get-tuple-element.85), channel_id=1, source_target_pairs={{0,4},{4,0},{1,5},{5,1},{2,6},{6,2},{3,7},{7,3},{8,12},{12,8},{9,1... | collective-permute-start | bytes 3145736 | tf_op jit(solution)/shard_map/ppermute | solution.py:40
  84.0 9.2 %collective-permute-start.10 = (bf16[64,2048]{1,0:T(8,128)(2,1)S(1)}, bf16[64,2048]{1,0:T(8,128)(2,1)S(1)}, u32[]{:S(2)}, u32[]{:S(2)}) collective-permute-start(bf16[64,2048]{1,0:T(8,128)(2,1)S(1)} %get-tuple-element.87), channel_id=1, source_target_pairs={{0,8},{8,0},{16,24},{24,16},{1,9},{9,1},{17,25},{25,17},{2,10},{10... | collective-permute-start | bytes 786440 | tf_op jit(solution)/shard_map/ppermute | solution.py:40
  85.6 13.7 %collective-permute-start.11 = (bf16[64,2048]{1,0:T(8,128)(2,1)S(1)}, bf16[64,2048]{1,0:T(8,128)(2,1)S(1)}, u32[]{:S(2)}, u32[]{:S(2)}) collective-permute-start(bf16[64,2048]{1,0:T(8,128)(2,1)S(1)} %get-tuple-element.88), channel_id=1, source_target_pairs={{0,16},{8,24},{16,0},{24,8},{1,17},{9,25},{17,1},{25,9},{2,18},{10... | collective-permute-start | bytes 786440 | tf_op jit(solution)/shard_map/ppermute | solution.py:40
  87.1 12.2 %collective-permute-start.12 = (bf16[64,2048]{1,0:T(8,128)(2,1)S(1)}, bf16[64,2048]{1,0:T(8,128)(2,1)S(1)}, u32[]{:S(2)}, u32[]{:S(2)}) collective-permute-start(bf16[64,2048]{1,0:T(8,128)(2,1)S(1)} %get-tuple-element.89), channel_id=1, source_target_pairs={{0,24},{8,16},{16,8},{24,0},{1,25},{9,17},{17,9},{25,1},{2,26},{10... | collective-permute-start | bytes 786440 | tf_op jit(solution)/shard_map/ppermute | solution.py:40
  99.4 10.2 %collective-permute-start.15 = (bf16[64,2048]{1,0:T(8,128)(2,1)S(1)}, bf16[64,2048]{1,0:T(8,128)(2,1)S(1)}, u32[]{:S(2)}, u32[]{:S(2)}) collective-permute-start(bf16[64,2048]{1,0:T(8,128)(2,1)S(1)} %scene_mean.1.refs_0_), channel_id=1, source_target_pairs={{0,24},{8,16},{16,8},{24,0},{1,25},{9,17},{17,9},{25,1},{2,26},{10... | collective-permute-start | bytes 786440 | tf_op jit(solution)/shard_map/ppermute | solution.py:40
  101.0 12.3 %collective-permute-start.14 = (bf16[64,2048]{1,0:T(8,128)(2,1)S(1)}, bf16[64,2048]{1,0:T(8,128)(2,1)S(1)}, u32[]{:S(2)}, u32[]{:S(2)}) collective-permute-start(bf16[64,2048]{1,0:T(8,128)(2,1)S(1)} %scene_mean.1.refs_0_), channel_id=1, source_target_pairs={{0,16},{8,24},{16,0},{24,8},{1,17},{9,25},{17,1},{25,9},{2,18},{10... | collective-permute-start | bytes 786440 | tf_op jit(solution)/shard_map/ppermute | solution.py:40
  102.2 11.1 %collective-permute-start.13 = (bf16[64,2048]{1,0:T(8,128)(2,1)S(1)}, bf16[64,2048]{1,0:T(8,128)(2,1)S(1)}, u32[]{:S(2)}, u32[]{:S(2)}) collective-permute-start(bf16[64,2048]{1,0:T(8,128)(2,1)S(1)} %scene_mean.1.refs_0_), channel_id=1, source_target_pairs={{0,8},{8,0},{16,24},{24,16},{1,9},{9,1},{17,25},{25,17},{2,10},{10... | collective-permute-start | bytes 786440 | tf_op jit(solution)/shard_map/ppermute | solution.py:40
  103.0 10.9 %collective-permute-start.16 = (bf16[64,2048]{1,0:T(8,128)(2,1)S(1)}, bf16[64,2048]{1,0:T(8,128)(2,1)S(1)}, u32[]{:S(2)}, u32[]{:S(2)}) collective-permute-start(bf16[64,2048]{1,0:T(8,128)(2,1)S(1)} %scene_mean.1.refs_0_), channel_id=1, source_target_pairs={{0,4},{4,0},{1,5},{5,1},{2,6},{6,2},{3,7},{7,3},{8,12},{12,8},{9,1... | collective-permute-start | bytes 786440 | tf_op jit(solution)/shard_map/ppermute | solution.py:40
  109.7 4.2 %collective-permute-start.19 = (bf16[64,2048]{1,0:T(8,128)(2,1)S(1)}, bf16[64,2048]{1,0:T(8,128)(2,1)S(1)}, u32[]{:S(2)}, u32[]{:S(2)}) collective-permute-start(bf16[64,2048]{1,0:T(8,128)(2,1)S(1)} %collective-permute-done.15.refs_3_), channel_id=1, source_target_pairs={{0,4},{4,0},{1,5},{5,1},{2,6},{6,2},{3,7},{7,3},{8,12},{12,8},{9,1... | collective-permute-start | bytes 786440 | tf_op jit(solution)/shard_map/ppermute | solution.py:40
  113.3 1.5 %collective-permute-start.18 = (bf16[64,2048]{1,0:T(8,128)(2,1)S(1)}, bf16[64,2048]{1,0:T(8,128)(2,1)S(1)}, u32[]{:S(2)}, u32[]{:S(2)}) collective-permute-start(bf16[64,2048]{1,0:T(8,128)(2,1)S(1)} %collective-permute-done.14.refs_2_), channel_id=1, source_target_pairs={{0,4},{4,0},{1,5},{5,1},{2,6},{6,2},{3,7},{7,3},{8,12},{12,8},{9,1... | collective-permute-start | bytes 786440 | tf_op jit(solution)/shard_map/ppermute | solution.py:40
  113.3 1.9 %collective-permute-start.17 = (bf16[64,2048]{1,0:T(8,128)(2,1)S(1)}, bf16[64,2048]{1,0:T(8,128)(2,1)S(1)}, u32[]{:S(2)}, u32[]{:S(2)}) collective-permute-start(bf16[64,2048]{1,0:T(8,128)(2,1)S(1)} %collective-permute-done.13.refs_1_), channel_id=1, source_target_pairs={{0,4},{4,0},{1,5},{5,1},{2,6},{6,2},{3,7},{7,3},{8,12},{12,8},{9,1... | collective-permute-start | bytes 786440 | tf_op jit(solution)/shard_map/ppermute | solution.py:40
where the time goes:
time: 119 us
  waiting for transfers between devices  61.6 us (52%)
  starting transfers between devices  29.1 us (24%)
  Pallas kernels  22.1 us (19%)
  local copies, waits for them, and re-layouts  4.18 us (4%)
  between operations  1.48 us (1%)
    ppermute x20, waiting for transfers between devices, swap(): return lax.ppermute(x, axis, [(i, i ^ flip) for i in range(size)])  61.6 us
    ppermute x20, starting transfers between devices, swap(): return lax.ppermute(x, axis, [(i, i ^ flip) for i in range(size)])  22.5 us
    pallas_call x9, Pallas kernels, whole(): pl.pallas_call(kernel, out_shape=out_shape, in_specs=[pl.BlockSpec(memory...  17.8 us
    all_to_all x1, starting transfers between devices, dense_body(): lax.all_to_all(back, 'shard', split_axis=0, concat_axis=0, tiled=True)  6.57 us
    unnamed x18, local copies, waits for them, and re-layouts  4.15 us
  transfers between devices with their start and end apart: 21, of which 11 were waited for; matrix products, arithmetic and copies ran while one was open for 0% of the time, Pallas kernels for 14%

commit v1 on v0

--- a/solution.py
+++ b/solution.py
@@ -65,10 +65,10 @@
     )(*operands)
 
 
-def pack_kernel(meta, q_ref, k_ref, v_ref, *refs):
+def pack_kernel(meta, q_ref, k_ref, v_ref, grad_ref, mine_ref, *refs):
     *outs, sems = refs
     width = outs[0].shape[2]
-    copies = []
+    copies = [pltpu.make_async_copy(grad_ref, mine_ref, sems.at[3 * len(outs)])]
     for n, out_ref in enumerate(outs):
         k, first = (n, 0) if n < 2 else (n // 2 + 1, n % 2 * EARLY * HDIM)
         start = pl.multiple_of((meta[Z] ^ k) * width + first, 128)
@@ -78,20 +78,21 @@
     run_all(copies)
 
 
-def pack(meta, queries, keys_in, values):
+def pack(meta, queries, keys_in, values, grad):
     rows, width = queries.shape
     part, early = width // 4, EARLY * HDIM
     shapes = [sds((3, rows, n), bf16) for n in (part, part, early, part - early, early, part - early)]
+    shapes = [sds(grad.shape, bf16)] + shapes
     return pl.pallas_call(
         pack_kernel,
         out_shape=shapes,
-        in_specs=[pl.BlockSpec(memory_space=pltpu.SMEM)] + [pl.BlockSpec(memory_space=pl.ANY)] * 3,
+        in_specs=[pl.BlockSpec(memory_space=pltpu.SMEM)] + [pl.BlockSpec(memory_space=pl.ANY)] * 4,
         out_specs=[pl.BlockSpec(memory_space=pltpu.VMEM)] * len(shapes),
         scratch_shapes=[pltpu.SemaphoreType.DMA((3 * len(shapes),))],
         compiler_params=params(),
         cost_estimate=NO_COST,
         name="pack_heads",
-    )(meta, queries, keys_in, values)
+    )(meta, queries, keys_in, values, grad)
 
 
 def token_pos(shape, dim, z, start=0):
@@ -205,20 +206,26 @@
 
 
 def backward_late_kernel(meta, *refs):
-    others, back_ref, own = refs[9:13], refs[13], refs[14:]
+    others, back_ref, own, sems = refs[9:13], refs[13], refs[14:18], refs[18]
+    part = others[0].shape[2]
+    copies = [
+        pltpu.make_async_copy(ref, back_ref.at[meta[Z] ^ k, :, :, pl.ds(0, part)], sems.at[k])
+        for k, ref in enumerate(others)
+    ]
+    for copy in copies:
+        copy.start()
     gradients(1, refs[:4], refs[4:6], refs[6:9], own)
-    first = others[0].shape[2]
-    for k in range(4):
-        place = meta[Z] ^ k
-        back_ref[place, :, :, :first] = others[k][...]
-        back_ref[place, :, :, first:] = own[k][...]
+    for k, ref in enumerate(own):
+        back_ref[meta[Z] ^ k, :, :, part:] = ref[...]
+    for copy in copies:
+        copy.wait()
 
 
 def backward_late(meta, pieces, grads, saved, others):
     _, rows, part = pieces[-1].shape
-    shape = sds((4, 3, rows, others[0].shape[2] + part), bf16)
+    shape = sds((4, *pieces[0].shape), bf16)
     operands = (meta, *pieces, *grads, *saved, *others)
-    scratch = [pltpu.VMEM((3, rows, part), bf16)] * 4
+    scratch = [pltpu.VMEM((3, rows, part), bf16)] * 4 + [pltpu.SemaphoreType.DMA((4,))]
     return whole(backward_late_kernel, shape, operands, "backward_late", 1, 16, scratch)
 
 
@@ -334,26 +341,26 @@
 
     across = send(out_grad, 2)
     beside = send(out_grad, 1)
-    own, near1, far2a, far2b, far3a, far3b = pack(meta, queries, keys_in, values)
+    mine, own, near1, far2a, far2b, far3a, far3b = pack(meta, queries, keys_in, values, out_grad)
     piece1 = send(near1, 1)
     piece3a = send(far3a, 3, beside)
     piece2a = send(far2a, 2, across)
     piece3b = send(far3b, 3, piece3a)
     piece2b = send(far2b, 2, piece2a)
     half = across.shape[0] // 2
-    corners = [send(across[:half], 1), send(after(across, piece1)[half:], 1)]
-    grad_early = grad_attn(meta, (out_grad, beside, across), out_weight, 0)
+    grad_early = grad_attn(meta, (mine, beside, across), out_weight, 0)
+    corners = [send(across[:half], 1), send(after(across, piece1, grad_early)[half:], 1)]
 
     pieces = (own, piece1, piece2a, piece3a)
     *saved, heads_a = forward(meta, pieces, 0)
     grad_early, heads_a, *corners = lax.optimization_barrier((grad_early, heads_a, *corners))
-    grads = (out_grad, beside, across, *corners)
+    grads = (mine, beside, across, *corners)
     grad_heads = (grad_early, grad_attn(meta, grads[3:], out_weight, 3 * BLOCK))
-    mine = backward_early(pieces, grad_heads, saved)
-    *mine, piece2b, piece3b = lax.optimization_barrier((*mine, piece2b, piece3b))
+    others = backward_early(pieces, grad_heads, saved)
+    *others, piece2b, piece3b = lax.optimization_barrier((*others, piece2b, piece3b))
     pieces = (own, piece1, piece2b, piece3b)
     *saved, heads_b = forward(meta, pieces, 1)
-    back = backward_late(meta, pieces, grad_heads, saved, mine)
+    back = backward_late(meta, pieces, grad_heads, saved, others)
     back_all = lax.all_to_all(back, "shard", split_axis=0, concat_axis=0, tiled=True)
 
     out, keep = weight_halves(meta, (heads_a, after(heads_b, back)), grads)
@@ -362,8 +369,9 @@
     done = total_of(own_part, recvs, 1.0 / 8)
     near = [done] + [swap(done, "chips", 4, j) for j in (1, 2, 3)]
     far = [swap(x, "core", 2, 1) for x in near]
-    grad_weight = join_weight(meta, near + far)
-    return (*join(back_all), grad_weight)
+    grads_in = join(back_all)
+    far[-1] = after(far[-1], grads_in[0])
+    return (*grads_in, join_weight(meta, near + far))
 
 
 def attend_listed(queries, keys_in, values, block_ids, live_count):

time: 119 us -> 119 us (level)
  waiting for transfers between devices: 61.6 us -> 58 us
  local copies, waits for them, and re-layouts: 4.18 us -> 6.17 us
  starting transfers between devices: 29.1 us -> 31 us
    ppermute x20, waiting for transfers between devices: 61.6 us -> 58 us  [swap(): return lax.ppermute(x, axis, [(i, i ^ flip) for i in range(size)])]
    unnamed x18 -> x22, local copies, waits for them, and re-layouts: 4.15 us -> 6.14 us
    all_to_all x1, starting transfers between devices: 6.57 us -> 7.87 us  [dense_body(): lax.all_to_all(back, 'shard', split_axis=0, concat_axis=0, tiled=True)]
  transfers between devices with their start and end apart: 21 -> 21, of which waited for: 11 -> 11; matrix products, arithmetic and copies ran while one was open for 0% -> 0% of each run, Pallas kernels for 14% -> 12%
where the time goes in v1:
time: 119 us; the launch traced here: 118 us
  waiting for transfers between devices  58 us (49%)
  starting transfers between devices  31 us (26%)
  Pallas kernels  21.6 us (18%)
  local copies, waits for them, and re-layouts  6.17 us (5%)
  between operations  1.49 us (1%)
    ppermute x20, waiting for transfers between devices, swap(): return lax.ppermute(x, axis, [(i, i ^ flip) for i in range(size)])  58 us
    ppermute x20, starting transfers between devices, swap(): return lax.ppermute(x, axis, [(i, i ^ flip) for i in range(size)])  23.1 us
    pallas_call x9, Pallas kernels, whole(): pl.pallas_call(kernel, out_shape=out_shape, in_specs=[pl.BlockSpec(memory...  16.8 us
    all_to_all x1, starting transfers between devices, dense_body(): lax.all_to_all(back, 'shard', split_axis=0, concat_axis=0, tiled=True)  7.87 us
    unnamed x22, local copies, waits for them, and re-layouts  6.14 us
    pallas_call x1, Pallas kernels, join_weight(): pl.pallas_call(join_weight_kernel, out_shape=sds((8 * size, outw), bf16),...  2.53 us
  transfers between devices with their start and end apart: 21, of which 11 were waited for; matrix products, arithmetic and copies ran while one was open for 0% of the time, Pallas kernels for 12%

profile of v1, /device:TPU:0, one launch (start us, length us, event | category | flops | bytes accessed | tf_op | source)
XLA Modules:
  0.0 118.4 jit_solution(17880750431257277623)
XLA Ops:
  0.6 3.1 %collective-permute-start.3 = (bf16[128,2048]{1,0:T(8,128)(2,1)}, bf16[128,2048]{1,0:T(8,128)(2,1)S(1)}, u32[]{:S(2)}, u32[]{:S(2)}) collective-permute-start(bf16[128,2048]{1,0:T(8,128)(2,1)} %grad_ref.1), channel_id=1, source_target_pairs={{0,1},{1,0},{2,3},{3,2},{4,5},{5,4},{6,7},{7,6},{8,9},{9,8},{10,11... | collective-permute-start | bytes 1572872 | tf_op jit(solution)/shard_map/ppermute | solution.py:40
  3.7 2.6 %collective-permute-start.1 = (bf16[128,2048]{1,0:T(8,128)(2,1)}, bf16[128,2048]{1,0:T(8,128)(2,1)S(1)}, u32[]{:S(2)}, u32[]{:S(2)}) collective-permute-start(bf16[128,2048]{1,0:T(8,128)(2,1)} %grad_ref.1), channel_id=1, source_target_pairs={{0,2},{1,3},{2,0},{3,1},{4,6},{5,7},{6,4},{7,5},{8,10},{9,11},{10,... | collective-permute-start | bytes 1572872 | tf_op jit(solution)/shard_map/ppermute | solution.py:40
  7.0 0.1 pad_add_fusion.meta
  7.1 1.0 copy-done.5
  8.1 1.0 copy-done.6
  9.1 1.0 copy-done.7
  10.2 1.0 copy-done.8
  11.2 1.1 pack_heads.1
  12.3 0.0 copy-start.1
  12.3 0.5 collective-permute-start
  12.8 15.0 %collective-permute-done.3.refs_1_ = bf16[128,2048]{1,0:T(8,128)(2,1)S(1)} collective-permute-done((bf16[128,2048]{1,0:T(8,128)(2,1)}, bf16[128,2048]{1,0:T(8,128)(2,1)S(1)}, u32[]{:S(2)}, u32[]{:S(2)}) %collective-permute-start.3) | collective-permute-done | bytes 524320 | tf_op jit(solution)/shard_map/ppermute | solution.py:40
  27.8 3.6 %collective-permute-start.4 = (bf16[3,128,384]{2,1,0:T(8,128)(2,1)S(1)}, bf16[3,128,384]{2,1,0:T(8,128)(2,1)S(1)}, u32[]{:S(2)}, u32[]{:S(2)}) collective-permute-start(bf16[3,128,384]{2,1,0:T(8,128)(2,1)S(1)} %get-tuple-element.54), channel_id=1, source_target_pairs={{0,3},{1,2},{2,1},{3,0},{4,7},{5,6},{6,5},{7,4},{8,11},{9,10},{10,... | collective-permute-start | bytes 884744 | tf_op jit(solution)/shard_map/ppermute | solution.py:40
  31.4 0.0 collective-permute-done.1.refs_2_
  31.4 0.0 collective-permute-start.2
  31.4 2.1 %collective-permute-start.5 = (bf16[64,2048]{1,0:T(8,128)(2,1)S(1)}, bf16[64,2048]{1,0:T(8,128)(2,1)S(1)}, u32[]{:S(2)}, u32[]{:S(2)}) collective-permute-start(bf16[64,2048]{1,0:T(8,128)(2,1)S(1)} %slice.8), channel_id=1, source_target_pairs={{0,1},{1,0},{2,3},{3,2},{4,5},{5,4},{6,7},{7,6},{8,9},{9,8},{10,11... | collective-permute-start | bytes 786440 | tf_op jit(solution)/shard_map/ppermute | solution.py:40
  33.5 1.9 %grad_attn.2.refs_4_ = bf16[384,512]{1,0:T(8,128)(2,1)S(1)} custom-call(s32[4]{0:T(128)S(1)} %pad_add_fusion.meta, bf16[128,2048]{1,0:T(8,128)(2,1)S(1)} %get-tuple-element.55.refs_0_, bf16[128,2048]{1,0:T(8,128)(2,1)S(1)} %collective-permute-done.3.refs_1_, bf16[128,2048]{1,0:T(8,128)(2,1)S(1)} %collective-permute-done.1.refs_2_, bf16[512,2048]{1,0:T(8,128)(2,1)S(1)} %copy-done), custom_call_target="tpu_custom_call" | custom-call | bytes 1024 | tf_op jit(solution)/shard_map/grad_attn/pallas_call | solution.py:55
  35.4 8.7 %collective-permute-done.p1.refs_1_ = bf16[3,128,512]{2,1,0:T(8,128)(2,1)S(1)} collective-permute-done((bf16[3,128,512]{2,1,0:T(8,128)(2,1)S(1)}, bf16[3,128,512]{2,1,0:T(8,128)(2,1)S(1)}, u32[]{:S(2)}, u32[]{:S(2)}) %collective-permute-start) | collective-permute-done | bytes 393248 | tf_op jit(solution)/shard_map/ppermute | solution.py:40
  44.1 0.1 collective-permute-start.6
  44.2 1.2 collective-permute-done.4.p3.refs_3_
  45.3 3.0 %collective-permute-start.8 = (bf16[3,128,128]{2,1,0:T(8,128)(2,1)S(1)}, bf16[3,128,128]{2,1,0:T(8,128)(2,1)S(1)}, u32[]{:S(2)}, u32[]{:S(2)}) collective-permute-start(bf16[3,128,128]{2,1,0:T(8,128)(2,1)S(1)} %get-tuple-element.71), channel_id=1, source_target_pairs={{0,3},{1,2},{2,1},{3,0},{4,7},{5,6},{6,5},{7,4},{8,11},{9,10},{10,... | collective-permute-start | bytes 294920 | tf_op jit(solution)/shard_map/ppermute | solution.py:40
  48.3 7.6 %collective-permute-done.2.p2.refs_2_ = bf16[3,128,384]{2,1,0:T(8,128)(2,1)S(1)} collective-permute-done((bf16[3,128,384]{2,1,0:T(8,128)(2,1)S(1)}, bf16[3,128,384]{2,1,0:T(8,128)(2,1)S(1)}, u32[]{:S(2)}, u32[]{:S(2)}) %collective-permute-start.2) | collective-permute-done | bytes 294944 | tf_op jit(solution)/shard_map/ppermute | solution.py:40
  55.9 0.0 collective-permute-start.7
  55.9 3.4 %attend_forward.2 = (bf16[3,512,512]{2,1,0:T(8,128)(2,1)S(1)}, f32[3,1,512]{2,1,0:T(1,128)S(1)}, f32[384,512]{1,0:T(8,128)S(1)}, bf16[384,512]{1,0:T(8,128)(2,1)S(1)}) custom-call(s32[4]{0:T(128)S(1)} %pad_add_fusion.meta, bf16[3,128,512]{2,1,0:T(8,128)(2,1)S(1)} %get-tuple-element.49.p0.refs_0_, bf16[3,128,512]{2,1,0:T(8,128)(2,1)S(1)} %collective-permute-done.p1.refs_1_, ...), custom_call_target="tpu_custom_call" | custom-call | bytes 1024 | tf_op jit(solution)/shard_map/attend_forward/pallas_call | solution.py:55
  59.3 0.0 copy-start.9
  59.3 0.0 collective-permute-done.5.refs_0_.refs_3_
  59.3 1.1 collective-permute-done.6.refs_1_.refs_4_
  60.5 1.6 %grad_attn.3.refs_5_ = bf16[128,512]{1,0:T(8,128)(2,1)S(1)} custom-call(s32[4]{0:T(128)S(1)} %pad_add_fusion.meta, bf16[64,2048]{1,0:T(8,128)(2,1)S(1)} %collective-permute-done.5.refs_0_.refs_3_, bf16[64,2048]{1,0:T(8,128)(2,1)S(1)} %collective-permute-done.6.refs_1_.refs_4_, bf16[512,2048]{1,0:T(8,128)(2,1)S(1)} %copy-done), custom_call_target="tpu_custom_call" | custom-call | bytes 1024 | tf_op jit(solution)/shard_map/grad_attn/pallas_call | solution.py:55
  62.0 2.8 %backward_early.1 = (bf16[3,128,384]{2,1,0:T(8,128)(2,1)S(1)}, bf16[3,128,384]{2,1,0:T(8,128)(2,1)S(1)}, bf16[3,128,384]{2,1,0:T(8,128)(2,1)S(1)}, bf16[3,128,384]{2,1,0:T(8,128)(2,1)S(1)}) custom-call(bf16[3,128,512]{2,1,0:T(8,128)(2,1)S(1)} %get-tuple-element.49.p0.refs_0_, bf16[3,128,512]{2,1,0:T(8,128)(2,1)S(1)} %collective-permute-done.p1.refs_1_, ...), custom_call_target="tpu_custom_call" | custom-call | bytes 1024 | tf_op jit(solution)/shard_map/backward_early/pallas_call | solution.py:55
  64.8 0.0 collective-permute-done.8.p3.refs_3_
  64.8 0.0 collective-permute-done.7.p2.refs_2_
  64.8 1.6 %attend_forward.3 = (bf16[1,512,512]{2,1,0:T(8,128)(2,1)S(1)}, f32[1,1,512]{2,1,0:T(1,128)S(1)}, f32[128,512]{1,0:T(8,128)S(1)}, bf16[128,512]{1,0:T(8,128)(2,1)S(1)}) custom-call(s32[4]{0:T(128)S(1)} %pad_add_fusion.meta, bf16[3,128,512]{2,1,0:T(8,128)(2,1)S(1)} %get-tuple-element.49.p0.refs_0_, bf16[3,128,512]{2,1,0:T(8,128)(2,1)S(1)} %collective-permute-done.p1.refs_1_, ...), custom_call_target="tpu_custom_call" | custom-call | bytes 1024 | tf_op jit(solution)/shard_map/attend_forward/pallas_call | solution.py:55
  66.5 2.9 %backward_late.1 = bf16[4,3,128,512]{3,2,1,0:T(8,128)(2,1)} custom-call(s32[4]{0:T(128)S(1)} %pad_add_fusion.meta, bf16[3,128,512]{2,1,0:T(8,128)(2,1)S(1)} %get-tuple-element.49.p0.refs_0_, bf16[3,128,512]{2,1,0:T(8,128)(2,1)S(1)} %collective-permute-done.p1.refs_1_, bf16[3,128,128]{2,1,0:T(8,128)(2,1)S(1)} %collective-permute-done.7.p2.refs_2_, ...), custom_call_target="tpu_custom_call" | custom-call | bytes 1024 | tf_op jit(solution)/shard_map/backward_late/pallas_call | solution.py:55
  69.4 0.0 copy-start.2
  69.4 7.9 %all-to-all-start = ((bf16[4,3,128,512]{3,2,1,0:T(8,128)(2,1)}), bf16[4,3,128,512]{3,2,1,0:T(8,128)(2,1)S(1)}, u32[]{:S(2)}, u32[]{:S(2)}) async-start(bf16[4,3,128,512]{3,2,1,0:T(8,128)(2,1)} %backward_late.1), calls=%async_computation | async-start | bytes 3145728 | tf_op jit(solution)/shard_map/all_to_all | solution.py:364
  77.3 0.9 copy-done.4
  78.3 1.0 copy-done.10
  79.3 2.4 %weight_halves.1 = (bf16[256,2048]{1,0:T(8,128)(2,1)S(1)}, f32[256,2048]{1,0:T(8,128)S(1)}) custom-call(s32[4]{0:T(128)S(1)} %pad_add_fusion.meta, bf16[384,512]{1,0:T(8,128)(2,1)S(1)} %copy-done.10, bf16[128,512]{1,0:T(8,128)(2,1)S(1)} %get-tuple-element.86.heads_b, bf16[128,2048]{1,0:T(8,128)(2,1)S(1)} %copy-done.2, ...), custom_call_target="tpu_custom_call" | custom-call | bytes 1024 | tf_op jit(solution)/shard_map/weight_halves/pallas_call | solution.py:55
  81.6 0.1 collective-permute-start.9
  81.7 2.6 %collective-permute-done.9.recv_ref = bf16[256,2048]{1,0:T(8,128)(2,1)S(1)} collective-permute-done((bf16[256,2048]{1,0:T(8,128)(2,1)S(1)}, bf16[256,2048]{1,0:T(8,128)(2,1)S(1)}, u32[]{:S(2)}, u32[]{:S(2)}) %collective-permute-start.9) | collective-permute-done | bytes 1048608 | tf_op jit(solution)/shard_map/ppermute | solution.py:40
  84.3 0.2 add_parts.1
  84.6 1.6 %collective-permute-start.10 = (bf16[64,2048]{1,0:T(8,128)(2,1)S(1)}, bf16[64,2048]{1,0:T(8,128)(2,1)S(1)}, u32[]{:S(2)}, u32[]{:S(2)}) collective-permute-start(bf16[64,2048]{1,0:T(8,128)(2,1)S(1)} %get-tuple-element.90), channel_id=1, source_target_pairs={{0,8},{8,0},{16,24},{24,16},{1,9},{9,1},{17,25},{25,17},{2,10},{10... | collective-permute-start | bytes 786440 | tf_op jit(solution)/shard_map/ppermute | solution.py:40
  86.1 1.5 %collective-permute-start.11 = (bf16[64,2048]{1,0:T(8,128)(2,1)S(1)}, bf16[64,2048]{1,0:T(8,128)(2,1)S(1)}, u32[]{:S(2)}, u32[]{:S(2)}) collective-permute-start(bf16[64,2048]{1,0:T(8,128)(2,1)S(1)} %get-tuple-element.91), channel_id=1, source_target_pairs={{0,16},{8,24},{16,0},{24,8},{1,17},{9,25},{17,1},{25,9},{2,18},{10... | collective-permute-start | bytes 786440 | tf_op jit(solution)/shard_map/ppermute | solution.py:40
  87.6 0.5 collective-permute-start.12
  88.1 5.7 %collective-permute-done.10.r1 = bf16[64,2048]{1,0:T(8,128)(2,1)S(1)} collective-permute-done((bf16[64,2048]{1,0:T(8,128)(2,1)S(1)}, bf16[64,2048]{1,0:T(8,128)(2,1)S(1)}, u32[]{:S(2)}, u32[]{:S(2)}) %collective-permute-start.10) | collective-permute-done | bytes 262176 | tf_op jit(solution)/shard_map/ppermute | solution.py:40
  93.8 6.0 %collective-permute-done.11.r2 = bf16[64,2048]{1,0:T(8,128)(2,1)S(1)} collective-permute-done((bf16[64,2048]{1,0:T(8,128)(2,1)S(1)}, bf16[64,2048]{1,0:T(8,128)(2,1)S(1)}, u32[]{:S(2)}, u32[]{:S(2)}) %collective-permute-start.11) | collective-permute-done | bytes 262176 | tf_op jit(solution)/shard_map/ppermute | solution.py:40
  99.8 0.0 collective-permute-done.12.r3
  99.8 0.1 scene_mean.1.refs_0_
  99.9 1.6 %collective-permute-start.15 = (bf16[64,2048]{1,0:T(8,128)(2,1)S(1)}, bf16[64,2048]{1,0:T(8,128)(2,1)S(1)}, u32[]{:S(2)}, u32[]{:S(2)}) collective-permute-start(bf16[64,2048]{1,0:T(8,128)(2,1)S(1)} %scene_mean.1.refs_0_), channel_id=1, source_target_pairs={{0,24},{8,16},{16,8},{24,0},{1,25},{9,17},{17,9},{25,1},{2,26},{10... | collective-permute-start | bytes 786440 | tf_op jit(solution)/shard_map/ppermute | solution.py:40
  101.5 1.2 %collective-permute-start.14 = (bf16[64,2048]{1,0:T(8,128)(2,1)S(1)}, bf16[64,2048]{1,0:T(8,128)(2,1)S(1)}, u32[]{:S(2)}, u32[]{:S(2)}) collective-permute-start(bf16[64,2048]{1,0:T(8,128)(2,1)S(1)} %scene_mean.1.refs_0_), channel_id=1, source_target_pairs={{0,16},{8,24},{16,0},{24,8},{1,17},{9,25},{17,1},{25,9},{2,18},{10... | collective-permute-start | bytes 786440 | tf_op jit(solution)/shard_map/ppermute | solution.py:40
  102.7 0.8 collective-permute-start.13
  103.5 6.7 %collective-permute-done.15.refs_3_ = bf16[64,2048]{1,0:T(8,128)(2,1)S(1)} collective-permute-done((bf16[64,2048]{1,0:T(8,128)(2,1)S(1)}, bf16[64,2048]{1,0:T(8,128)(2,1)S(1)}, u32[]{:S(2)}, u32[]{:S(2)}) %collective-permute-start.15) | collective-permute-done | bytes 262176 | tf_op jit(solution)/shard_map/ppermute | solution.py:40
  110.2 0.0 collective-permute-start.19
  110.2 0.5 collective-permute-start.16
  110.7 3.1 %collective-permute-done.14.refs_2_ = bf16[64,2048]{1,0:T(8,128)(2,1)S(1)} collective-permute-done((bf16[64,2048]{1,0:T(8,128)(2,1)S(1)}, bf16[64,2048]{1,0:T(8,128)(2,1)S(1)}, u32[]{:S(2)}, u32[]{:S(2)}) %collective-permute-start.14) | collective-permute-done | bytes 262176 | tf_op jit(solution)/shard_map/ppermute | solution.py:40
  113.8 0.0 collective-permute-start.18
  113.8 0.0 collective-permute-done.13.refs_1_
  113.8 0.5 collective-permute-start.17
  114.3 0.0 all-to-all-done.back_ref
  114.3 1.2 %join_heads.1 = (bf16[128,2048]{1,0:T(8,128)(2,1)}, bf16[128,2048]{1,0:T(8,128)(2,1)}, bf16[128,2048]{1,0:T(8,128)(2,1)}) custom-call(bf16[4,3,128,512]{3,2,1,0:T(8,128)(2,1)S(1)} %all-to-all-done.back_ref), custom_call_target="tpu_custom_call" | custom-call | bytes 1024 | tf_op jit(solution)/shard_map/join_heads/pallas_call | solution.py:323
  115.6 0.0 collective-permute-done.19.refs_7_
  115.6 0.0 collective-permute-done.16.refs_4_
  115.6 0.0 collective-permute-done.18.refs_6_
  115.6 0.3 collective-permute-done.17.refs_5_
  115.9 2.5 %join_weight.1 = bf16[512,2048]{1,0:T(8,128)(2,1)} custom-call(s32[4]{0:T(128)S(1)} %pad_add_fusion.meta, bf16[64,2048]{1,0:T(8,128)(2,1)S(1)} %scene_mean.1.refs_0_, bf16[64,2048]{1,0:T(8,128)(2,1)S(1)} %collective-permute-done.13.refs_1_, bf16[64,2048]{1,0:T(8,128)(2,1)S(1)} %collective-permute-done.14.refs_2_, ...), custom_call_target="tpu_custom_call" | custom-call | bytes 1024 | tf_op jit(solution)/shard_map/join_weight/pallas_call | solution.py:298
  (15 shorter events, 0.1 us)
Async XLA Ops:
  0.6 32.9 %copy-start = (bf16[512,2048]{1,0:T(8,128)(2,1)S(1)}, bf16[512,2048]{1,0:T(8,128)(2,1)}, u32[]{:S(2)}) copy-start(bf16[512,2048]{1,0:T(8,128)(2,1)} %refs_2_.1) | copy-start | bytes 6291460
  0.6 27.2 %collective-permute-start.3 = (bf16[128,2048]{1,0:T(8,128)(2,1)}, bf16[128,2048]{1,0:T(8,128)(2,1)S(1)}, u32[]{:S(2)}, u32[]{:S(2)}) collective-permute-start(bf16[128,2048]{1,0:T(8,128)(2,1)} %grad_ref.1), channel_id=1, source_target_pairs={{0,1},{1,0},{2,3},{3,2},{4,5},{5,4},{6,7},{7,6},{8,9},{9,8},{10,11... | collective-permute-start | bytes 1572872 | tf_op jit(solution)/shard_map/ppermute | solution.py:40
  3.7 27.7 %collective-permute-start.1 = (bf16[128,2048]{1,0:T(8,128)(2,1)}, bf16[128,2048]{1,0:T(8,128)(2,1)S(1)}, u32[]{:S(2)}, u32[]{:S(2)}) collective-permute-start(bf16[128,2048]{1,0:T(8,128)(2,1)} %grad_ref.1), channel_id=1, source_target_pairs={{0,2},{1,3},{2,0},{3,1},{4,6},{5,7},{6,4},{7,5},{8,10},{9,11},{10,... | collective-permute-start | bytes 1572872 | tf_op jit(solution)/shard_map/ppermute | solution.py:40
  7.0 1.0 copy-start.5
  8.1 1.0 copy-start.6
  9.1 1.0 copy-start.7
  10.2 1.0 copy-start.8
  12.3 23.1 %copy-start.1 = (bf16[128,2048]{1,0:T(8,128)(2,1)}, bf16[128,2048]{1,0:T(8,128)(2,1)S(1)}, u32[]{:S(2)}) copy-start(bf16[128,2048]{1,0:T(8,128)(2,1)S(1)} %get-tuple-element.55.refs_0_) | copy-start | bytes 1572868
  12.3 31.8 %collective-permute-start = (bf16[3,128,512]{2,1,0:T(8,128)(2,1)S(1)}, bf16[3,128,512]{2,1,0:T(8,128)(2,1)S(1)}, u32[]{:S(2)}, u32[]{:S(2)}) collective-permute-start(bf16[3,128,512]{2,1,0:T(8,128)(2,1)S(1)} %get-tuple-element.50), channel_id=1, source_target_pairs={{0,1},{1,0},{2,3},{3,2},{4,5},{5,4},{6,7},{7,6},{8,9},{9,8},{10,11... | collective-permute-start | bytes 1179656 | tf_op jit(solution)/shard_map/ppermute | solution.py:40
  27.8 17.5 %collective-permute-start.4 = (bf16[3,128,384]{2,1,0:T(8,128)(2,1)S(1)}, bf16[3,128,384]{2,1,0:T(8,128)(2,1)S(1)}, u32[]{:S(2)}, u32[]{:S(2)}) collective-permute-start(bf16[3,128,384]{2,1,0:T(8,128)(2,1)S(1)} %get-tuple-element.54), channel_id=1, source_target_pairs={{0,3},{1,2},{2,1},{3,0},{4,7},{5,6},{6,5},{7,4},{8,11},{9,10},{10,... | collective-permute-start | bytes 884744 | tf_op jit(solution)/shard_map/ppermute | solution.py:40
  31.4 24.5 %collective-permute-start.2 = (bf16[3,128,384]{2,1,0:T(8,128)(2,1)S(1)}, bf16[3,128,384]{2,1,0:T(8,128)(2,1)S(1)}, u32[]{:S(2)}, u32[]{:S(2)}) collective-permute-start(bf16[3,128,384]{2,1,0:T(8,128)(2,1)S(1)} %get-tuple-element.52), channel_id=1, source_target_pairs={{0,2},{1,3},{2,0},{3,1},{4,6},{5,7},{6,4},{7,5},{8,10},{9,11},{10,... | collective-permute-start | bytes 884744 | tf_op jit(solution)/shard_map/ppermute | solution.py:40
  31.4 27.9 %collective-permute-start.5 = (bf16[64,2048]{1,0:T(8,128)(2,1)S(1)}, bf16[64,2048]{1,0:T(8,128)(2,1)S(1)}, u32[]{:S(2)}, u32[]{:S(2)}) collective-permute-start(bf16[64,2048]{1,0:T(8,128)(2,1)S(1)} %slice.8), channel_id=1, source_target_pairs={{0,1},{1,0},{2,3},{3,2},{4,5},{5,4},{6,7},{7,6},{8,9},{9,8},{10,11... | collective-permute-start | bytes 786440 | tf_op jit(solution)/shard_map/ppermute | solution.py:40
  44.1 16.4 %collective-permute-start.6 = (bf16[64,2048]{1,0:T(8,128)(2,1)S(1)}, bf16[64,2048]{1,0:T(8,128)(2,1)S(1)}, u32[]{:S(2)}, u32[]{:S(2)}) collective-permute-start(bf16[64,2048]{1,0:T(8,128)(2,1)S(1)} %slice.7), channel_id=1, source_target_pairs={{0,1},{1,0},{2,3},{3,2},{4,5},{5,4},{6,7},{7,6},{8,9},{9,8},{10,11... | collective-permute-start | bytes 786440 | tf_op jit(solution)/shard_map/ppermute | solution.py:40
  45.3 19.5 %collective-permute-start.8 = (bf16[3,128,128]{2,1,0:T(8,128)(2,1)S(1)}, bf16[3,128,128]{2,1,0:T(8,128)(2,1)S(1)}, u32[]{:S(2)}, u32[]{:S(2)}) collective-permute-start(bf16[3,128,128]{2,1,0:T(8,128)(2,1)S(1)} %get-tuple-element.71), channel_id=1, source_target_pairs={{0,3},{1,2},{2,1},{3,0},{4,7},{5,6},{6,5},{7,4},{8,11},{9,10},{10,... | collective-permute-start | bytes 294920 | tf_op jit(solution)/shard_map/ppermute | solution.py:40
  55.9 8.9 %collective-permute-start.7 = (bf16[3,128,128]{2,1,0:T(8,128)(2,1)S(1)}, bf16[3,128,128]{2,1,0:T(8,128)(2,1)S(1)}, u32[]{:S(2)}, u32[]{:S(2)}) collective-permute-start(bf16[3,128,128]{2,1,0:T(8,128)(2,1)S(1)} %get-tuple-element.69), channel_id=1, source_target_pairs={{0,2},{1,3},{2,0},{3,1},{4,6},{5,7},{6,4},{7,5},{8,10},{9,11},{10,... | collective-permute-start | bytes 294920 | tf_op jit(solution)/shard_map/ppermute | solution.py:40
  59.3 5.5 %copy-start.9 = (bf16[384,512]{1,0:T(8,128)(2,1)}, bf16[384,512]{1,0:T(8,128)(2,1)S(1)}, u32[]{:S(2)}) copy-start(bf16[384,512]{1,0:T(8,128)(2,1)S(1)} %get-tuple-element.84.heads_a) | copy-start | bytes 1179652
  60.5 4.3 %copy-start.3 = (bf16[64,2048]{1,0:T(8,128)(2,1)}, bf16[64,2048]{1,0:T(8,128)(2,1)S(1)}, u32[]{:S(2)}) copy-start(bf16[64,2048]{1,0:T(8,128)(2,1)S(1)} %collective-permute-done.6.refs_1_.refs_4_) | copy-start | bytes 786436
  69.4 7.9 %copy-start.2 = (bf16[128,2048]{1,0:T(8,128)(2,1)S(1)}, bf16[128,2048]{1,0:T(8,128)(2,1)}, u32[]{:S(2)}) copy-start(bf16[128,2048]{1,0:T(8,128)(2,1)} %copy-done.1) | copy-start | bytes 1572868
  69.4 44.9 %all-to-all-start = ((bf16[4,3,128,512]{3,2,1,0:T(8,128)(2,1)}), bf16[4,3,128,512]{3,2,1,0:T(8,128)(2,1)S(1)}, u32[]{:S(2)}, u32[]{:S(2)}) async-start(bf16[4,3,128,512]{3,2,1,0:T(8,128)(2,1)} %backward_late.1), calls=%async_computation | async-start | bytes 3145728 | tf_op jit(solution)/shard_map/all_to_all | solution.py:364
  77.3 1.0 copy-start.4
  78.3 1.0 copy-start.10
  81.6 2.7 %collective-permute-start.9 = (bf16[256,2048]{1,0:T(8,128)(2,1)S(1)}, bf16[256,2048]{1,0:T(8,128)(2,1)S(1)}, u32[]{:S(2)}, u32[]{:S(2)}) collective-permute-start(bf16[256,2048]{1,0:T(8,128)(2,1)S(1)} %get-tuple-element.88), channel_id=1, source_target_pairs={{0,4},{4,0},{1,5},{5,1},{2,6},{6,2},{3,7},{7,3},{8,12},{12,8},{9,1... | collective-permute-start | bytes 3145736 | tf_op jit(solution)/shard_map/ppermute | solution.py:40
  84.6 9.2 %collective-permute-start.10 = (bf16[64,2048]{1,0:T(8,128)(2,1)S(1)}, bf16[64,2048]{1,0:T(8,128)(2,1)S(1)}, u32[]{:S(2)}, u32[]{:S(2)}) collective-permute-start(bf16[64,2048]{1,0:T(8,128)(2,1)S(1)} %get-tuple-element.90), channel_id=1, source_target_pairs={{0,8},{8,0},{16,24},{24,16},{1,9},{9,1},{17,25},{25,17},{2,10},{10... | collective-permute-start | bytes 786440 | tf_op jit(solution)/shard_map/ppermute | solution.py:40
  86.1 13.7 %collective-permute-start.11 = (bf16[64,2048]{1,0:T(8,128)(2,1)S(1)}, bf16[64,2048]{1,0:T(8,128)(2,1)S(1)}, u32[]{:S(2)}, u32[]{:S(2)}) collective-permute-start(bf16[64,2048]{1,0:T(8,128)(2,1)S(1)} %get-tuple-element.91), channel_id=1, source_target_pairs={{0,16},{8,24},{16,0},{24,8},{1,17},{9,25},{17,1},{25,9},{2,18},{10... | collective-permute-start | bytes 786440 | tf_op jit(solution)/shard_map/ppermute | solution.py:40
  87.6 12.2 %collective-permute-start.12 = (bf16[64,2048]{1,0:T(8,128)(2,1)S(1)}, bf16[64,2048]{1,0:T(8,128)(2,1)S(1)}, u32[]{:S(2)}, u32[]{:S(2)}) collective-permute-start(bf16[64,2048]{1,0:T(8,128)(2,1)S(1)} %get-tuple-element.92), channel_id=1, source_target_pairs={{0,24},{8,16},{16,8},{24,0},{1,25},{9,17},{17,9},{25,1},{2,26},{10... | collective-permute-start | bytes 786440 | tf_op jit(solution)/shard_map/ppermute | solution.py:40
  99.9 10.2 %collective-permute-start.15 = (bf16[64,2048]{1,0:T(8,128)(2,1)S(1)}, bf16[64,2048]{1,0:T(8,128)(2,1)S(1)}, u32[]{:S(2)}, u32[]{:S(2)}) collective-permute-start(bf16[64,2048]{1,0:T(8,128)(2,1)S(1)} %scene_mean.1.refs_0_), channel_id=1, source_target_pairs={{0,24},{8,16},{16,8},{24,0},{1,25},{9,17},{17,9},{25,1},{2,26},{10... | collective-permute-start | bytes 786440 | tf_op jit(solution)/shard_map/ppermute | solution.py:40
  101.5 12.3 %collective-permute-start.14 = (bf16[64,2048]{1,0:T(8,128)(2,1)S(1)}, bf16[64,2048]{1,0:T(8,128)(2,1)S(1)}, u32[]{:S(2)}, u32[]{:S(2)}) collective-permute-start(bf16[64,2048]{1,0:T(8,128)(2,1)S(1)} %scene_mean.1.refs_0_), channel_id=1, source_target_pairs={{0,16},{8,24},{16,0},{24,8},{1,17},{9,25},{17,1},{25,9},{2,18},{10... | collective-permute-start | bytes 786440 | tf_op jit(solution)/shard_map/ppermute | solution.py:40
  102.7 11.1 %collective-permute-start.13 = (bf16[64,2048]{1,0:T(8,128)(2,1)S(1)}, bf16[64,2048]{1,0:T(8,128)(2,1)S(1)}, u32[]{:S(2)}, u32[]{:S(2)}) collective-permute-start(bf16[64,2048]{1,0:T(8,128)(2,1)S(1)} %scene_mean.1.refs_0_), channel_id=1, source_target_pairs={{0,8},{8,0},{16,24},{24,16},{1,9},{9,1},{17,25},{25,17},{2,10},{10... | collective-permute-start | bytes 786440 | tf_op jit(solution)/shard_map/ppermute | solution.py:40
  110.2 5.4 %collective-permute-start.19 = (bf16[64,2048]{1,0:T(8,128)(2,1)S(1)}, bf16[64,2048]{1,0:T(8,128)(2,1)S(1)}, u32[]{:S(2)}, u32[]{:S(2)}) collective-permute-start(bf16[64,2048]{1,0:T(8,128)(2,1)S(1)} %collective-permute-done.15.refs_3_), channel_id=1, source_target_pairs={{0,4},{4,0},{1,5},{5,1},{2,6},{6,2},{3,7},{7,3},{8,12},{12,8},{9,1... | collective-permute-start | bytes 786440 | tf_op jit(solution)/shard_map/ppermute | solution.py:40
  110.2 5.4 %collective-permute-start.16 = (bf16[64,2048]{1,0:T(8,128)(2,1)S(1)}, bf16[64,2048]{1,0:T(8,128)(2,1)S(1)}, u32[]{:S(2)}, u32[]{:S(2)}) collective-permute-start(bf16[64,2048]{1,0:T(8,128)(2,1)S(1)} %scene_mean.1.refs_0_), channel_id=1, source_target_pairs={{0,4},{4,0},{1,5},{5,1},{2,6},{6,2},{3,7},{7,3},{8,12},{12,8},{9,1... | collective-permute-start | bytes 786440 | tf_op jit(solution)/shard_map/ppermute | solution.py:40
  113.8 1.8 %collective-permute-start.18 = (bf16[64,2048]{1,0:T(8,128)(2,1)S(1)}, bf16[64,2048]{1,0:T(8,128)(2,1)S(1)}, u32[]{:S(2)}, u32[]{:S(2)}) collective-permute-start(bf16[64,2048]{1,0:T(8,128)(2,1)S(1)} %collective-permute-done.14.refs_2_), channel_id=1, source_target_pairs={{0,4},{4,0},{1,5},{5,1},{2,6},{6,2},{3,7},{7,3},{8,12},{12,8},{9,1... | collective-permute-start | bytes 786440 | tf_op jit(solution)/shard_map/ppermute | solution.py:40
  113.8 2.0 %collective-permute-start.17 = (bf16[64,2048]{1,0:T(8,128)(2,1)S(1)}, bf16[64,2048]{1,0:T(8,128)(2,1)}, u32[]{:S(2)}, u32[]{:S(2)}) collective-permute-start(bf16[64,2048]{1,0:T(8,128)(2,1)S(1)} %collective-permute-done.13.refs_1_), channel_id=1, source_target_pairs={{0,4},{4,0},{1,5},{5,1},{2,6},{6,2},{3,7},{7,3},{8,12},{12,8},{9,1... | collective-permute-start | bytes 786440 | tf_op jit(solution)/shard_map/ppermute | solution.py:40
